TPU v7x, 256 devices: a whole 4x4x8 slice. The times are simulated.
256 devices in a mesh: chain: 32 (over y_hi, z, core), mp: 8 (over y_lo, x).
Axes of the slice: x: 4, y: 4 (y_hi: 2, y_lo: 2; y = y_hi * 2 + y_lo), z: 8, core: 2. Of those that a mesh axis runs over, the one named last changes fastest.
Arguments:
- latents: float32 [1, 128, 4, 40, 64], P(None, 'chain', None, 'mp'), may hold values from -6 to 6
- step_noise: float32 [1, 128, 4, 40, 64], P(None, 'chain', None, 'mp'), may hold values from -6 to 6
- fresh_noise: float32 [1, 4, 40, 64], P(None, None, 'mp'), may hold values from -6 to 6
- timesteps: int32 [128], P('chain'), may hold values from 0 to 999
- step_coefs: float32 [3, 128], P(None, 'chain'), may hold values from -0.7 to 1.15
- inlet_weight: bfloat16 [9, 4, 320], replicated, may hold values from -1 to 1
- time_first: bfloat16 [320, 1280], replicated, may hold values from -0.3125 to 0.3125
- time_second: bfloat16 [1280, 320], replicated, may hold values from -0.15625 to 0.15625
- res_weight: bfloat16 [9, 320, 320], replicated, may hold values from -0.109375 to 0.109375
- query_weight: bfloat16 [320, 320], replicated, may hold values from -1.35 to 1.35
- key_weight: bfloat16 [320, 320], replicated, may hold values from -1.35 to 1.35
- value_weight: bfloat16 [320, 320], replicated, may hold values from -0.3125 to 0.3125
- output_weight: bfloat16 [320, 320], replicated, may hold values from -0.3125 to 0.3125
- outlet_weight: bfloat16 [9, 320, 4], replicated, may hold values from -0.109375 to 0.109375
Outputs:
- stepped: float32 [1, 128, 4, 40, 64], P(None, 'chain', None, 'mp')
- advanced: float32 [1, 128, 4, 40, 64], P(None, 'chain', None, 'mp')
All inputs are finite; a program needn't handle non-finite values.
Results may differ from a plain program's by a relative error of at most 0.0029.
Values may be sent and summed in bfloat16 or wider, within the bound.
No kernel may reach another device: no remote copies, remote signals or barrier semaphores. Data moves between devices by JAX's collectives and lax.ppermute only.
A program may use at most 128 MiB of HBM per device.

v0:
```python
import math

import jax
import jax.numpy as jnp
from jax import lax
from jax.sharding import PartitionSpec as P

HEAD_DIM = 64
WINDOW = 16


def extended_2(block, sides, width):
    for axis, dim in sides:
        count = lax.axis_size(axis)
        forward = [(i, i + 1) for i in range(count - 1)]
        backward = [(target, source) for source, target in forward]
        low = lax.ppermute(
            lax.slice_in_dim(block, block.shape[dim] - width, None, axis=dim), axis, forward
        )
        high = lax.ppermute(lax.slice_in_dim(block, 0, width, axis=dim), axis, backward)
        block = jnp.concatenate([low, block, high], axis=dim)
    return block


def from_partner(block, axis, bit):
    count = lax.axis_size(axis)
    route = []
    for low in range(count):
        high = low | 1 << bit
        if high != low and high < count:
            route += [(low, high), (high, low)]
    return lax.ppermute(block, axis, route)


def passed_along(array, axis, by):
    size = lax.axis_size(axis)
    pairs = [(i, i + by) for i in range(size) if 0 <= i + by < size]
    return lax.ppermute(array, axis, pairs)


def embed_steps(timesteps, channels):
    half_dim = channels // 2
    frequency = jnp.exp(-math.log(10000.0) * jnp.arange(half_dim, dtype=jnp.float32) / half_dim)
    angles = timesteps.astype(jnp.float32)[:, None] * frequency[None, :]
    return jnp.concatenate([jnp.cos(angles), jnp.sin(angles)], axis=1)


def rms_normed(hidden):
    return hidden * lax.rsqrt(jnp.mean(hidden * hidden, axis=-1, keepdims=True) + 1e-05)


def conv_taps(padded, weight):
    height = padded.shape[2] - 2
    lane_count = padded.shape[3]
    widened = jnp.pad(padded, ((0, 0), (0, 0), (0, 0), (1, 1), (0, 0)))
    summed = None
    for tap_index in range(9):
        tap_row = tap_index // 3
        tap_col = tap_index % 3
        window = widened[:, :, tap_row : tap_row + height, tap_col : tap_col + lane_count, :]
        term = jnp.einsum(
            "pfhwc,cd->pfhwd", window, weight[tap_index], preferred_element_type=jnp.float32
        )
        summed = term if summed is None else summed + term
    return summed


def local(
    latents,
    step_noise,
    fresh_noise,
    timesteps,
    step_coefs,
    inlet_weight,
    time_first,
    time_second,
    res_weight,
    query_weight,
    key_weight,
    value_weight,
    output_weight,
    outlet_weight,
):
    prompts, frames, lat_ch, height, lane_count = latents.shape
    channels = query_weight.shape[0]
    heads = channels // HEAD_DIM
    group_size = WINDOW // frames
    bit_count = group_size.bit_length() - 1
    embedded = embed_steps(timesteps, channels).astype(jnp.bfloat16)
    time_hidden = jax.nn.silu(
        jnp.dot(embedded, time_first, preferred_element_type=jnp.float32)
    ).astype(jnp.bfloat16)
    time_shift = jnp.dot(time_hidden, time_second, preferred_element_type=jnp.float32)
    latent_in = jnp.transpose(latents, (0, 1, 3, 4, 2)).astype(jnp.bfloat16)
    latent_pad = extended_2(latent_in, (("mp", 2),), 1)
    opening = conv_taps(latent_pad, inlet_weight)
    activated = jax.nn.silu(rms_normed(opening) + time_shift[None, :, None, None, :]).astype(
        jnp.bfloat16
    )
    active_pad = extended_2(activated, (("mp", 2),), 1)
    residual = opening + conv_taps(active_pad, res_weight)
    cell_count = height * lane_count
    normed = (
        rms_normed(residual).astype(jnp.bfloat16).reshape(prompts, frames, cell_count, channels)
    )
    queries = jnp.einsum(
        "pfsc,cd->pfsd", normed, query_weight, preferred_element_type=jnp.float32
    ).astype(jnp.bfloat16)
    kv_weight = jnp.concatenate([key_weight, value_weight], axis=1)
    extended = jnp.einsum(
        "pfsc,cd->pfsd", normed, kv_weight, preferred_element_type=jnp.float32
    ).astype(jnp.bfloat16)
    for bit in range(bit_count):
        partner = from_partner(extended, "chain", bit)
        extended = jnp.concatenate([extended, partner], axis=1)
    ext_frames = extended.shape[1]
    key_heads = extended[..., :channels].reshape(prompts, ext_frames, cell_count, heads, HEAD_DIM)
    value_heads = extended[..., channels:].reshape(prompts, ext_frames, cell_count, heads, HEAD_DIM)
    query_heads = queries.reshape(prompts, frames, cell_count, heads, HEAD_DIM)
    scores = jnp.einsum(
        "pfshd,pgshd->pfshg", query_heads, key_heads, preferred_element_type=jnp.float32
    ) / math.sqrt(HEAD_DIM)
    highest = jnp.max(scores, axis=-1, keepdims=True)
    expsum = jnp.exp(scores - highest)
    probs = (expsum / jnp.sum(expsum, axis=-1, keepdims=True)).astype(jnp.bfloat16)
    summed = jnp.einsum(
        "pfshg,pgshd->pfshd", probs, value_heads, preferred_element_type=jnp.float32
    )
    attended = summed.reshape(prompts, frames, cell_count, channels).astype(jnp.bfloat16)
    mixture = residual + jnp.einsum(
        "pfsc,cd->pfsd", attended, output_weight, preferred_element_type=jnp.float32
    ).reshape(prompts, frames, height, lane_count, channels)
    pre_out = jax.nn.silu(rms_normed(mixture)).astype(jnp.bfloat16)
    outer_pad = extended_2(pre_out, (("mp", 2),), 1)
    predicted = jnp.transpose(conv_taps(outer_pad, outlet_weight), (0, 1, 4, 2, 3))

    def per_slot(row_index):
        return step_coefs[row_index][None, :, None, None, None]

    stepped = per_slot(0) * latents + per_slot(1) * predicted + per_slot(2) * step_noise
    head_frame = stepped[:, :1]
    arrived = passed_along(head_frame, "chain", -1)
    is_last = lax.axis_index("chain") == lax.axis_size("chain") - 1
    tail_frame = jnp.where(is_last, fresh_noise[:, None], arrived)
    advanced = jnp.concatenate([stepped[:, 1:], tail_frame], axis=1)
    return (stepped, advanced)


def solution(mesh):
    return jax.shard_map(
        local,
        mesh=mesh,
        in_specs=(
            P(None, "chain", None, "mp", None),
            P(None, "chain", None, "mp", None),
            P(None, None, "mp", None),
            P("chain"),
            P(None, "chain"),
            P(),
            P(),
            P(),
            P(),
            P(),
            P(),
            P(),
            P(),
            P(),
        ),
        out_specs=(P(None, "chain", None, "mp", None), P(None, "chain", None, "mp", None)),
        check_vma=False,
    )
```

profile of v0, /device:TPU:231, one launch (start us, length us, event | category | flops | bytes accessed | tf_op | source)
XLA Modules:
  0.0 224.5 jit_solution(15954852719759467850)
XLA Ops:
  0.7 0.9 convert_bitcast_fusion
  1.5 3.1 %collective-permute-start = (bf16[1,4,1,64,4]{3,4,2,1,0:T(4,128)(2,1)S(1)}, bf16[1,4,1,64,4]{3,4,2,1,0:T(4,128)(2,1)S(1)}, u32[]{:S(2)}, u32[]{:S(2)}) collective-permute-start(bf16[1,4,1,64,4]{3,4,2,1,0:T(4,128)(2,1)S(1)} %get-tuple-element.8), channel_id=1, source_target_pairs={{0,1},{1,2},{2,3},{3,4},{4,5},{5,6},{6,7},{8,9},{9,10},{10,11},{11... | collective-permute-start | bytes 6152 | tf_op jit(solution)/shard_map/ppermute | solution.py:17
  4.7 2.2 collective-permute-start.1
  6.9 1.3 fusion.90
  8.3 1.7 fusion.93
  9.9 1.2 collective-permute-done.1
  11.2 0.6 fusion.77
  12.3 0.6 fusion.82
  13.4 0.6 fusion.84
  14.0 0.5 fusion.89
  15.0 1.4 multiply_reduce_fusion.2
  16.5 0.6 fusion.172
  17.2 4.1 %collective-permute-start.2 = (bf16[1,4,1,64,320]{4,3,2,1,0:T(8,128)(2,1)S(1)}, bf16[1,4,1,64,320]{4,3,2,1,0:T(8,128)(2,1)S(1)}, u32[]{:S(2)}, u32[]{:S(2)}) collective-permute-start(bf16[1,4,1,64,320]{4,3,2,1,0:T(8,128)(2,1)S(1)} %get-tuple-element.6), channel_id=1, source_target_pairs={{0,1},{1,2},{2,3},{3,4},{4,5},{5,6},{6,7},{8,9},{9,10},{10,11},{11... | collective-permute-start | bytes 491528 | tf_op jit(solution)/shard_map/ppermute | solution.py:17
  21.2 2.1 collective-permute-start.3
  23.4 1.0 fusion.60
  24.4 5.7 %collective-permute-done.3 = bf16[1,4,1,64,320]{4,3,2,1,0:T(8,128)(2,1)S(1)} collective-permute-done((bf16[1,4,1,64,320]{4,3,2,1,0:T(8,128)(2,1)S(1)}, bf16[1,4,1,64,320]{4,3,2,1,0:T(8,128)(2,1)S(1)}, u32[]{:S(2)}, u32[]{:S(2)}) %collective-permute-start.3) | collective-permute-done | bytes 163872 | tf_op jit(solution)/shard_map/ppermute | solution.py:20
  30.1 0.8 fusion.10
  30.9 0.7 fusion.40
  31.6 0.7 fusion.44
  32.4 0.7 fusion.45
  33.1 0.7 fusion.46
  33.9 0.7 fusion.47
  34.6 0.7 fusion.52
  35.4 0.7 fusion.49
  36.1 1.6 multiply_reduce_fusion.1
  38.1 0.7 copy-done.6
  38.9 1.1 fusion.14
  40.0 2.5 %collective-permute-start.4 = (bf16[1,4,320,640]{3,2,1,0:T(8,128)(2,1)S(1)}, bf16[1,4,320,640]{3,2,1,0:T(8,128)(2,1)S(1)}, u32[]{:S(2)}, u32[]{:S(2)}) collective-permute-start(bf16[1,4,320,640]{3,2,1,0:T(8,128)(2,1)S(1)} %fusion.14), channel_id=1, source_target_pairs={{0,8},{8,0},{16,24},{24,16},{32,40},{40,32},{48,56},{56,48},{64,72... | collective-permute-start | bytes 4915208 | tf_op jit(solution)/shard_map/ppermute | solution.py:32
  42.5 3.1 %collective-permute-done.4 = bf16[1,4,320,640]{3,2,1,0:T(8,128)(2,1)S(1)} collective-permute-done((bf16[1,4,320,640]{3,2,1,0:T(8,128)(2,1)S(1)}, bf16[1,4,320,640]{3,2,1,0:T(8,128)(2,1)S(1)}, u32[]{:S(2)}, u32[]{:S(2)}) %collective-permute-start.4) | collective-permute-done | bytes 1638432 | tf_op jit(solution)/shard_map/ppermute | solution.py:32
  45.7 2.2 pad_maximum_fusion.1
  47.9 0.7 collective-permute-start.5
  48.6 1.7 convolution_convert_fusion.2
  50.3 4.5 %copy.24 = bf16[4,320,5,64]{3,0,2,1:T(4,128)(2,1)} copy(bf16[4,320,5,64]{1,3,2,0:T(8,128)(2,1)} %bitcast.369) | data formatting | bytes 1638400 | tf_op jit(solution)/shard_map/reshape.54
  54.8 65.5 %collective-permute-done.5 = bf16[1,8,320,640]{3,2,1,0:T(8,128)(2,1)} collective-permute-done((bf16[1,8,320,640]{3,2,1,0:T(8,128)(2,1)}, bf16[1,8,320,640]{3,2,1,0:T(8,128)(2,1)}, u32[]{:S(2)}, u32[]{:S(2)}) %collective-permute-start.5) | collective-permute-done | bytes 3276832 | tf_op jit(solution)/shard_map/ppermute | solution.py:32
  120.3 3.8 %pad_maximum_fusion = bf16[1,16,320,640]{3,2,1,0:T(8,128)(2,1)S(1)} fusion(bf16[1,8,320,640]{3,2,1,0:T(8,128)(2,1)} %collective-permute-done.5, bf16[1,4,320,640]{3,2,1,0:T(8,128)(2,1)} %copy-done.4, bf16[1,4,320,640]{3,2,1,0:T(8,128)(2,1)} %copy-done.2), kind=kLoop, calls=%fused_computation | loop fusion | flops 6553600 | bytes 13107200 | tf_op jit(solution)/shard_map/concatenate | solution.py:115
  124.1 4.4 %fusion.157 = (bf16[1,16,320,320]{3,2,1,0:T(8,128)(2,1)}, bf16[1,16,320,320]{3,2,1,0:T(8,128)(2,1)}) fusion(bf16[1,16,320,640]{3,2,1,0:T(8,128)(2,1)S(1)} %pad_maximum_fusion), kind=kLoop, calls=%fused_computation.205 | loop fusion | bytes 13107200 | tf_op jit(solution)/shard_map/slice | solution.py:117
  128.5 6.2 %copy.21 = bf16[1,16,320,320]{2,3,1,0:T(8,128)(2,1)} copy(bf16[1,16,320,320]{3,2,1,0:T(8,128)(2,1)} %get-tuple-element.2) | data formatting | bytes 6553600 | tf_op jit(solution)/shard_map/slice | solution.py:117
  134.6 13.9 %copy.23 = bf16[16,320,5,64]{3,0,2,1:T(8,128)(2,1)} copy(bf16[16,320,5,64]{1,3,2,0:T(8,128)(2,1)} %bitcast.365) | data formatting | bytes 6553600 | tf_op jit(solution)/shard_map/reshape.53
  148.6 6.1 %copy.20 = bf16[1,16,320,320]{2,3,1,0:T(8,128)(2,1)} copy(bf16[1,16,320,320]{3,2,1,0:T(8,128)(2,1)} %get-tuple-element.3) | data formatting | bytes 6553600 | tf_op jit(solution)/shard_map/slice | solution.py:118
  154.7 13.9 %copy.25 = bf16[16,320,5,64]{3,0,2,1:T(8,128)(2,1)} copy(bf16[16,320,5,64]{1,3,2,0:T(8,128)(2,1)} %bitcast.366) | data formatting | bytes 6553600 | tf_op jit(solution)/shard_map/reshape.58
  168.6 8.6 %bitcast_reduce_fusion = (f32[4,320,5]{0,2,1:T(8,128)S(1)}, f32[320,5,16,4]{2,3,1,0:T(4,128)}) fusion(bf16[16,320,5,64]{3,0,2,1:T(8,128)(2,1)} %copy.23, bf16[4,320,5,64]{3,0,2,1:T(4,128)(2,1)} %copy.24), kind=kOutput, calls=%fused_computation.5 | convolution fusion | flops 13305600 | bytes 4531200 | tf_op jit(solution)/shard_map/pfshd,pgshd->pfshg/dot_general | solution.py:120
  177.2 5.4 %fusion.2 = f32[4,320,5]{0,2,1:T(8,128)S(1)} fusion(f32[320,5,16,4]{2,3,1,0:T(4,128)} %get-tuple-element.20, f32[4,320,5]{0,2,1:T(8,128)S(1)} %get-tuple-element.19), kind=kLoop, calls=%fused_computation.9 | loop fusion | flops 300800 | bytes 460800 | tf_op jit(solution)/shard_map/reduce_sum | solution.py:125
  182.6 6.7 %fusion.11 = bf16[1,4,320,5,64]{4,1,3,2,0:T(4,128)(2,1)S(1)} fusion(bf16[16,320,5,64]{3,0,2,1:T(8,128)(2,1)} %copy.25, f32[4,320,5]{0,2,1:T(8,128)S(1)} %fusion.2, f32[320,5,16,4]{2,3,1,0:T(4,128)S(1)} %copy-done.3, f32[4,320,5]{0,2,1:T(8,128)S(1)} %get-tuple-element.19), kind=kOutput, calls=%fused_computation.31 | convolution fusion | flops 13926400 | bytes 4556800 | tf_op jit(solution)/shard_map/pfshg,pgshd->pfshd/dot_general | solution.py:126
  189.3 2.0 copy.26
  191.3 4.2 %convert_element_type.77 = bf16[4,5,64,320]{3,2,1,0:T(8,128)(2,1)} reshape(bf16[1,4,320,5,64]{4,3,2,1,0:T(8,128)(2,1)} %copy.26) | data formatting | bytes 1638400 | tf_op jit(solution)/shard_map/convert_element_type | solution.py:129
  195.5 2.1 multiply_reduce_fusion
  197.6 0.6 fusion.171
  198.2 1.9 collective-permute-start.6
  200.2 3.4 %collective-permute-start.7 = (bf16[1,4,1,64,320]{4,3,2,1,0:T(8,128)(2,1)S(1)}, bf16[1,4,1,64,320]{4,3,2,1,0:T(8,128)(2,1)S(1)}, u32[]{:S(2)}, u32[]{:S(2)}) collective-permute-start(bf16[1,4,1,64,320]{4,3,2,1,0:T(8,128)(2,1)S(1)} %get-tuple-element.5), channel_id=1, source_target_pairs={{1,0},{2,1},{3,2},{4,3},{5,4},{6,5},{7,6},{9,8},{10,9},{11,10},{12... | collective-permute-start | bytes 491528 | tf_op jit(solution)/shard_map/ppermute | solution.py:20
  203.5 0.8 fusion.113
  204.3 1.0 collective-permute-done.6
  205.3 4.0 %collective-permute-done.7 = bf16[1,4,1,64,320]{4,3,2,1,0:T(8,128)(2,1)S(1)} collective-permute-done((bf16[1,4,1,64,320]{4,3,2,1,0:T(8,128)(2,1)S(1)}, bf16[1,4,1,64,320]{4,3,2,1,0:T(8,128)(2,1)S(1)}, u32[]{:S(2)}, u32[]{:S(2)}) %collective-permute-start.7) | collective-permute-done | bytes 163872 | tf_op jit(solution)/shard_map/ppermute | solution.py:20
  209.4 0.8 select_maximum_fusion
  210.1 0.6 fusion.29
  210.7 0.6 fusion.30
  211.4 0.6 fusion.23
  212.0 0.6 fusion.28
  212.6 0.6 fusion.32
  213.2 0.6 fusion.39
  213.9 0.6 fusion.25
  214.5 0.7 fusion.22
  215.2 4.0 %collective-permute-start.8 = (f32[1,1,4,5,64]{4,2,3,1,0:T(4,128)S(1)}, f32[1,1,4,5,64]{4,2,3,1,0:T(4,128)S(1)}, u32[]{:S(2)}, u32[]{:S(2)}) collective-permute-start(f32[1,1,4,5,64]{4,2,3,1,0:T(4,128)S(1)} %slice.301), channel_id=1, source_target_pairs={{8,0},{16,8},{24,16},{32,24},{40,32},{48,40},{56,48},{64,56},{72,6... | collective-permute-start | bytes 15368 | tf_op jit(solution)/shard_map/ppermute | solution.py:38
  219.3 4.6 %collective-permute-done.8 = f32[1,1,4,5,64]{4,2,3,1,0:T(4,128)S(1)} collective-permute-done((f32[1,1,4,5,64]{4,2,3,1,0:T(4,128)S(1)}, f32[1,1,4,5,64]{4,2,3,1,0:T(4,128)S(1)}, u32[]{:S(2)}, u32[]{:S(2)}) %collective-permute-start.8) | collective-permute-done | bytes 5152 | tf_op jit(solution)/shard_map/ppermute | solution.py:38
  223.8 0.6 pad_maximum_fusion.6
  (55 shorter events, 2.2 us)
Async XLA Ops:
  0.6 7.6 %copy-start = (bf16[1280,320]{0,1:T(8,128)(2,1)S(1)}, bf16[1280,320]{0,1:T(8,128)(2,1)}, u32[]{:S(2)}) copy-start(bf16[1280,320]{0,1:T(8,128)(2,1)} %param.21) | copy-start | bytes 2457604
  0.6 10.6 %copy-start.12 = (bf16[9,4,320]{2,1,0:T(4,128)(2,1)S(1)}, bf16[9,4,320]{2,1,0:T(4,128)(2,1)}, u32[]{:S(2)}) copy-start(bf16[9,4,320]{2,1,0:T(4,128)(2,1)} %param.19) | copy-start | bytes 69124
  0.7 7.5 %copy-start.17 = (s32[4]{0:T(128)S(1)}, s32[4]{0:T(128)}, u32[]{:S(2)}) copy-start(s32[4]{0:T(128)} %param.17) | copy-start | bytes 52
  1.5 8.4 %collective-permute-start = (bf16[1,4,1,64,4]{3,4,2,1,0:T(4,128)(2,1)S(1)}, bf16[1,4,1,64,4]{3,4,2,1,0:T(4,128)(2,1)S(1)}, u32[]{:S(2)}, u32[]{:S(2)}) collective-permute-start(bf16[1,4,1,64,4]{3,4,2,1,0:T(4,128)(2,1)S(1)} %get-tuple-element.8), channel_id=1, source_target_pairs={{0,1},{1,2},{2,3},{3,4},{4,5},{5,6},{6,7},{8,9},{9,10},{10,11},{11... | collective-permute-start | bytes 6152 | tf_op jit(solution)/shard_map/ppermute | solution.py:17
  4.7 6.5 %collective-permute-start.1 = (bf16[1,4,1,64,4]{3,4,2,1,0:T(4,128)(2,1)S(1)}, bf16[1,4,1,64,4]{3,4,2,1,0:T(4,128)(2,1)S(1)}, u32[]{:S(2)}, u32[]{:S(2)}) collective-permute-start(bf16[1,4,1,64,4]{3,4,2,1,0:T(4,128)(2,1)S(1)} %get-tuple-element.9), channel_id=1, source_target_pairs={{1,0},{2,1},{3,2},{4,3},{5,4},{6,5},{7,6},{9,8},{10,9},{11,10},{12... | collective-permute-start | bytes 6152 | tf_op jit(solution)/shard_map/ppermute | solution.py:20
  16.4 6.9 %copy-start.5 = (bf16[9,320,320]{2,1,0:T(8,128)(2,1)S(1)}, bf16[9,320,320]{2,1,0:T(8,128)(2,1)}, u32[]{:S(2)}) copy-start(bf16[9,320,320]{2,1,0:T(8,128)(2,1)} %param.22) | copy-start | bytes 5529604
  17.2 7.2 %collective-permute-start.2 = (bf16[1,4,1,64,320]{4,3,2,1,0:T(8,128)(2,1)S(1)}, bf16[1,4,1,64,320]{4,3,2,1,0:T(8,128)(2,1)S(1)}, u32[]{:S(2)}, u32[]{:S(2)}) collective-permute-start(bf16[1,4,1,64,320]{4,3,2,1,0:T(8,128)(2,1)S(1)} %get-tuple-element.6), channel_id=1, source_target_pairs={{0,1},{1,2},{2,3},{3,4},{4,5},{5,6},{6,7},{8,9},{9,10},{10,11},{11... | collective-permute-start | bytes 491528 | tf_op jit(solution)/shard_map/ppermute | solution.py:17
  21.2 8.9 %collective-permute-start.3 = (bf16[1,4,1,64,320]{4,3,2,1,0:T(8,128)(2,1)S(1)}, bf16[1,4,1,64,320]{4,3,2,1,0:T(8,128)(2,1)S(1)}, u32[]{:S(2)}, u32[]{:S(2)}) collective-permute-start(bf16[1,4,1,64,320]{4,3,2,1,0:T(8,128)(2,1)S(1)} %get-tuple-element.7), channel_id=1, source_target_pairs={{1,0},{2,1},{3,2},{4,3},{5,4},{6,5},{7,6},{9,8},{10,9},{11,10},{12... | collective-permute-start | bytes 491528 | tf_op jit(solution)/shard_map/ppermute | solution.py:20
  37.8 0.9 copy-start.6
  37.8 1.1 copy-start.7
  40.0 7.9 %copy-start.2 = (bf16[1,4,320,640]{3,2,1,0:T(8,128)(2,1)}, bf16[1,4,320,640]{3,2,1,0:T(8,128)(2,1)S(1)}, u32[]{:S(2)}) copy-start(bf16[1,4,320,640]{3,2,1,0:T(8,128)(2,1)S(1)} %fusion.14) | copy-start | bytes 4915204
  40.0 8.6 %copy-start.14 = (f32[3,4]{1,0:T(4,128)S(1)}, f32[3,4]{1,0:T(4,128)}, u32[]{:S(2)}) copy-start(f32[3,4]{1,0:T(4,128)} %param.18) | copy-start | bytes 148
  40.0 8.6 %copy-start.8 = (bf16[320,320]{1,0:T(8,128)(2,1)S(1)}, bf16[320,320]{1,0:T(8,128)(2,1)}, u32[]{:S(2)}) copy-start(bf16[320,320]{1,0:T(8,128)(2,1)} %param.23) | copy-start | bytes 614404
  40.0 5.7 %collective-permute-start.4 = (bf16[1,4,320,640]{3,2,1,0:T(8,128)(2,1)S(1)}, bf16[1,4,320,640]{3,2,1,0:T(8,128)(2,1)S(1)}, u32[]{:S(2)}, u32[]{:S(2)}) collective-permute-start(bf16[1,4,320,640]{3,2,1,0:T(8,128)(2,1)S(1)} %fusion.14), channel_id=1, source_target_pairs={{0,8},{8,0},{16,24},{24,16},{32,40},{40,32},{48,56},{56,48},{64,72... | collective-permute-start | bytes 4915208 | tf_op jit(solution)/shard_map/ppermute | solution.py:32
  45.7 2.2 copy-start.4
  47.9 72.4 %collective-permute-start.5 = (bf16[1,8,320,640]{3,2,1,0:T(8,128)(2,1)}, bf16[1,8,320,640]{3,2,1,0:T(8,128)(2,1)}, u32[]{:S(2)}, u32[]{:S(2)}) collective-permute-start(bf16[1,8,320,640]{3,2,1,0:T(8,128)(2,1)} %pad_maximum_fusion.1), channel_id=1, source_target_pairs={{0,16},{16,0},{8,24},{24,8},{32,48},{48,32},{40,56},{56,40},{64,80... | collective-permute-start | bytes 9830408 | tf_op jit(solution)/shard_map/ppermute | solution.py:32
  177.2 5.4 %copy-start.3 = (f32[320,5,16,4]{2,3,1,0:T(4,128)S(1)}, f32[320,5,16,4]{2,3,1,0:T(4,128)}, u32[]{:S(2)}) copy-start(f32[320,5,16,4]{2,3,1,0:T(4,128)} %get-tuple-element.20) | copy-start | bytes 1228804
  191.3 4.2 %copy-start.9 = (bf16[320,320]{1,0:T(8,128)(2,1)S(1)}, bf16[320,320]{1,0:T(8,128)(2,1)}, u32[]{:S(2)}) copy-start(bf16[320,320]{1,0:T(8,128)(2,1)} %param.26) | copy-start | bytes 614404
  197.5 6.0 %copy-start.16 = (bf16[9,320,4]{1,2,0:T(4,128)(2,1)S(1)}, bf16[9,320,4]{1,2,0:T(4,128)(2,1)}, u32[]{:S(2)}) copy-start(bf16[9,320,4]{1,2,0:T(4,128)(2,1)} %param.27) | copy-start | bytes 69124
  198.2 7.1 %collective-permute-start.6 = (bf16[1,4,1,64,320]{4,3,2,1,0:T(8,128)(2,1)S(1)}, bf16[1,4,1,64,320]{4,3,2,1,0:T(8,128)(2,1)S(1)}, u32[]{:S(2)}, u32[]{:S(2)}) collective-permute-start(bf16[1,4,1,64,320]{4,3,2,1,0:T(8,128)(2,1)S(1)} %get-tuple-element.4), channel_id=1, source_target_pairs={{0,1},{1,2},{2,3},{3,4},{4,5},{5,6},{6,7},{8,9},{9,10},{10,11},{11... | collective-permute-start | bytes 491528 | tf_op jit(solution)/shard_map/ppermute | solution.py:17
  200.2 9.2 %collective-permute-start.7 = (bf16[1,4,1,64,320]{4,3,2,1,0:T(8,128)(2,1)S(1)}, bf16[1,4,1,64,320]{4,3,2,1,0:T(8,128)(2,1)S(1)}, u32[]{:S(2)}, u32[]{:S(2)}) collective-permute-start(bf16[1,4,1,64,320]{4,3,2,1,0:T(8,128)(2,1)S(1)} %get-tuple-element.5), channel_id=1, source_target_pairs={{1,0},{2,1},{3,2},{4,3},{5,4},{6,5},{7,6},{9,8},{10,9},{11,10},{12... | collective-permute-start | bytes 491528 | tf_op jit(solution)/shard_map/ppermute | solution.py:20
  212.6 1.9 copy-start.10
  212.6 1.9 copy-start.15
  213.2 11.2 %copy-start.1 = (bf16[1280,320]{0,1:T(8,128)(2,1)S(1)}, bf16[1280,320]{0,1:T(8,128)(2,1)}, u32[]{:S(2)}) copy-start(bf16[1280,320]{0,1:T(8,128)(2,1)} %param.21) | copy-start | bytes 2457604
  213.9 9.9 %copy-start.13 = (f32[1,4,5,64]{3,1,2,0:T(4,128)S(1)}, f32[1,4,5,64]{3,1,2,0:T(4,128)}, u32[]{:S(2)}) copy-start(f32[1,4,5,64]{3,1,2,0:T(4,128)} %param.16) | copy-start | bytes 15364
  215.2 9.3 %copy-start.11 = (f32[1,4,4,5,64]{4,2,3,1,0:T(4,128)}, f32[1,4,4,5,64]{4,2,3,1,0:T(4,128)S(1)}, u32[]{:S(2)}) copy-start(f32[1,4,4,5,64]{4,2,3,1,0:T(4,128)S(1)} %fusion.22) | copy-start | bytes 61444
  215.2 8.6 %collective-permute-start.8 = (f32[1,1,4,5,64]{4,2,3,1,0:T(4,128)S(1)}, f32[1,1,4,5,64]{4,2,3,1,0:T(4,128)S(1)}, u32[]{:S(2)}, u32[]{:S(2)}) collective-permute-start(f32[1,1,4,5,64]{4,2,3,1,0:T(4,128)S(1)} %slice.301), channel_id=1, source_target_pairs={{8,0},{16,8},{24,16},{32,24},{40,32},{48,40},{56,48},{64,56},{72,6... | collective-permute-start | bytes 15368 | tf_op jit(solution)/shard_map/ppermute | solution.py:38
where the time goes:
time: 226 us; the launch traced here: 224 us
  waiting for transfers between devices  85.2 us (38%)
  local copies, waits for them, and re-layouts  56.1 us (25%)
  matrix products  41.9 us (19%)
  starting transfers between devices  24 us (11%)
  other arithmetic  16.1 us (7%)
    ppermute x2, waiting for transfers between devices, from_partner(): return lax.ppermute(block, axis, route)  68.7 us
    another operation x3, local copies, waits for them, and re-layouts  32.3 us
    dot_general x27, matrix products, conv_taps(): jnp.einsum('pfhwc,cd->pfhwd', window, weight[tap_index], preferred_elemen...  20.1 us
    ppermute x3, waiting for transfers between devices, extended_2(): lax.ppermute(lax.slice_in_dim(block, 0, width, axis=dim), axis, backward)  10.9 us
    slice x2, local copies, waits for them, and re-layouts, local(): extended[..., :channels]  10.6 us
    ppermute x3, starting transfers between devices, extended_2(): lax.ppermute(lax.slice_in_dim(block, block.shape[dim] - width, None, axis...  9.12 us
    dot_general x1, matrix products, local(): jnp.einsum('pfshd,pgshd->pfshg', query_heads, key_heads, preferred_elemen...  8.58 us
    ppermute x3, starting transfers between devices, extended_2(): lax.ppermute(lax.slice_in_dim(block, 0, width, axis=dim), axis, backward)  7.63 us
  transfers between devices with their start and end apart: 9, of which 7 were waited for; matrix products, arithmetic and copies ran while one was open for 5% of the time, Pallas kernels for 0%

commit v1 on v0

v1 whole, which is shorter than its diff:
```python
import functools
import math

import jax
import jax.numpy as jnp
from jax import lax
from jax.experimental import pallas as pl
from jax.experimental.pallas import tpu as pltpu
from jax.sharding import PartitionSpec as P

F32 = jnp.float32
BF16 = jnp.bfloat16
HEADS = 5
HEAD_DIM = 64
C = 320
GROUP = 4


def from_partner(block, bits):
    count = lax.axis_size("chain")
    return lax.ppermute(block, "chain", [(i, i ^ bits) for i in range(count)])


def from_row(block, by):
    count = lax.axis_size("mp")
    pairs = [(i, i + by) for i in range(count) if 0 <= i + by < count]
    return lax.ppermute(block, "mp", pairs)


def embed_steps(timesteps):
    half_dim = C // 2
    frequency = jnp.exp(-math.log(10000.0) * jnp.arange(half_dim, dtype=F32) / half_dim)
    angles = timesteps.astype(F32)[:, None] * frequency[None, :]
    return jnp.concatenate([jnp.cos(angles), jnp.sin(angles)], axis=1)


def halved_silu(half):
    return half * jnp.tanh(half) + half


def inv_rms(values):
    return lax.rsqrt(jnp.sum(values * values, axis=0, keepdims=True) * (1.0 / C) + 1e-05)


def iota(shape, dim):
    return lax.broadcasted_iota(jnp.int32, shape, dim)


def core_kernel(
    s0, s1, s2, s3, win, wres, wqkv, wo, wout, o0, o1, o2, o3, act, opn, accs
):
    tile = lax.axis_index("chain") % GROUP
    row_block = lax.axis_index("mp")
    slabs = [s0[...], s1[...], s2[...], s3[...]]
    shift_rows = jnp.concatenate([s[80:112] for s in slabs], axis=0)
    er, el = iota((128, 640), 0), iota((128, 640), 1)
    pick = (er % 32 // 4 == el // 128) & (er // 32 * 4 + er % 4 == el % 128 // 8)
    spread = lax.dot_general(
        shift_rows.astype(F32).T.astype(BF16),
        pick.astype(F32).astype(BF16),
        (((1,), (0,)), ((), ())),
        preferred_element_type=F32,
    )
    spread = spread[:64] + spread[64:]
    shift = jnp.concatenate([spread[:, 128 * i : 128 * i + 128] for i in range(5)], axis=0) * 0.5
    latent = jnp.concatenate([s[:80] for s in slabs], axis=0)
    lane = iota((128, 384), 1)
    cell, slot, block = lane % 8, lane % 128 // 8, lane // 128
    at = jnp.where(
        block < 2,
        16 * tile + 8 * block + cell,
        jnp.where(cell == 0, 16 * tile - 1, jnp.where(cell == 7, 16 * tile + 16, -1000)),
    )
    src = iota((128, 384), 0)
    same_half = src // 64 == slot % 2
    pair_of = iota((1, 1, 384), 2) % 128 // 16
    pair_no = iota((8, 1, 384), 0)
    columns = []
    for dx in range(3):
        chosen = same_half & (src % 64 == at + (dx - 1))
        moved = jnp.dot(latent, chosen.astype(F32).astype(BF16), preferred_element_type=F32)
        moved = jnp.where(pair_of == pair_no, moved.reshape(8, 40, 384), 0.0)
        columns.append(jnp.sum(moved, axis=0))
    columns.append(jnp.zeros((8, 384), F32))
    columns = jnp.concatenate(columns, axis=0).astype(BF16)
    lane1 = iota((1, 128), 1)
    cell1 = lane1 % 8
    first, last = cell1 == 0, cell1 == 7
    side = jnp.where(
        first & (tile > 0), 1.0, jnp.where(last & (tile < GROUP - 1), 1.0, 0.0)
    )
    rows = lax.axis_size("mp")
    win_f = win[...].astype(F32)
    for r in range(7):
        weight = win_f if r == 0 else pltpu.roll(win_f, r, 1)
        opening = jnp.dot(weight.astype(BF16), columns, preferred_element_type=F32)
        if 1 <= r <= 5:
            opn[r - 1] = opening[:, :256]
        scale = inv_rms(opening) * 0.5
        parts = []
        for t in range(3):
            piece = slice(128 * t, 128 * t + 128)
            part = halved_silu(opening[:, piece] * scale[:, piece] + shift)
            if t == 2:
                part = part * side
            if r == 0:
                part = part * jnp.where(row_block > 0, 1.0, 0.0)
            if r == 6:
                part = part * jnp.where(row_block < rows - 1, 1.0, 0.0)
            parts.append(part)
        a0, a1, edge = parts
        base = 960 * r
        act[base : base + 320, :128] = jnp.where(first, edge, pltpu.roll(a0, 1, 1)).astype(BF16)
        act[base : base + 320, 128:] = jnp.where(
            first, pltpu.roll(a0, 121, 1), pltpu.roll(a1, 1, 1)
        ).astype(BF16)
        act[base + 320 : base + 640, :128] = a0.astype(BF16)
        act[base + 320 : base + 640, 128:] = a1.astype(BF16)
        act[base + 640 : base + 960, :128] = jnp.where(
            last, pltpu.roll(a1, 7, 1), pltpu.roll(a0, 127, 1)
        ).astype(BF16)
        act[base + 640 : base + 960, 128:] = jnp.where(
            last, edge, pltpu.roll(a1, 127, 1)
        ).astype(BF16)
    accs[...] = jnp.zeros_like(accs)
    same_cell = iota((8, 128), 0) == iota((8, 128), 1) % 8
    log2e8 = math.log2(math.e) / math.sqrt(HEAD_DIM)
    for r in range(5):
        residual = opn[r] + jnp.dot(
            wres[...], act[960 * r : 960 * r + 2880, :], preferred_element_type=F32
        )
        normed = (residual * inv_rms(residual)).astype(BF16)
        qkv = jnp.dot(wqkv[...], normed, preferred_element_type=F32).astype(BF16)
        blocks = []
        for b in range(2):
            piece = slice(128 * b, 128 * b + 128)
            heads = []
            for h in range(HEADS):
                query = qkv[64 * h : 64 * h + 64, piece]
                key = qkv[320 + 64 * h : 384 + 64 * h, piece]
                value = qkv[640 + 64 * h : 704 + 64 * h, piece]
                scores = lax.dot_general(
                    key, query, (((0,), (0,)), ((), ())), preferred_element_type=F32
                ).reshape(16, 8, 128)
                highest = jnp.max(scores, axis=0)
                expd = jnp.exp2((scores - highest) * log2e8)
                share = jnp.where(same_cell, 1.0 / jnp.sum(expd, axis=0), 0.0)
                probs = (expd * share).reshape(128, 128).astype(BF16)
                heads.append(jnp.dot(value, probs, preferred_element_type=F32).astype(BF16))
            blocks.append(jnp.concatenate(heads, axis=0))
        attended = jnp.concatenate(blocks, axis=1)
        mixture = residual + jnp.dot(wo[...], attended, preferred_element_type=F32)
        pre_out = halved_silu(mixture * (0.5 * inv_rms(mixture))).astype(BF16)
        taps = jnp.dot(wout[...], pre_out, preferred_element_type=F32)
        for a in range(3):
            accs[r + 2 - a] += taps[16 * a : 16 * a + 16]
    src = iota((256, 128), 0)
    dst = iota((256, 128), 1)
    same_half = src % 128 // 8 % 2 == dst // 64
    spot = 16 * tile + src // 128 * 8 + src % 8 - dst % 64
    pair_of = iota((1, 1, 256), 2) % 128 // 16
    pair_no = iota((8, 1, 256), 0)
    total = None
    for b in range(3):
        chosen = (same_half & (spot == b - 1)).astype(F32).astype(BF16)
        part = jnp.concatenate([accs[:, 4 * b + ch, :] for ch in range(4)], axis=0)
        high = part.astype(BF16).astype(F32)
        for piece in (high, part - high):
            wide = jnp.where(pair_of == pair_no, piece[None], 0.0)
            term = jnp.dot(
                wide.reshape(256, 256).astype(BF16), chosen, preferred_element_type=F32
            )
            total = term if total is None else total + term
    for k, out in enumerate((o0, o1, o2, o3)):
        out[...] = total[64 * k : 64 * k + 64].astype(BF16)


def core(slabs, win, wres, wqkv, wo, wout):
    out = jax.ShapeDtypeStruct((64, 128), BF16)
    vmem = pl.BlockSpec(memory_space=pltpu.VMEM)
    return pl.pallas_call(
        core_kernel,
        out_shape=(out,) * 4,
        in_specs=[vmem] * 9,
        out_specs=(vmem,) * 4,
        scratch_shapes=[
            pltpu.VMEM((7 * 960, 256), BF16),
            pltpu.VMEM((5, 320, 256), F32),
            pltpu.VMEM((8, 16, 256), F32),
        ],
        compiler_params=pltpu.CompilerParams(vmem_limit_bytes=48 * 1024 * 1024),
        cost_estimate=pl.CostEstimate(
            flops=4_000_000_000, bytes_accessed=3_000_000, transcendentals=3_000_000
        ),
    )(*slabs, win, wres, wqkv, wo, wout)


def local(
    latents,
    step_noise,
    fresh_noise,
    timesteps,
    step_coefs,
    inlet_weight,
    time_first,
    time_second,
    res_weight,
    query_weight,
    key_weight,
    value_weight,
    output_weight,
    outlet_weight,
):
    latent = latents[0]
    narrow = latent.astype(BF16)
    below = from_row(narrow[:, :, 3:], 1)
    above = from_row(narrow[:, :, :2], -1)
    embedded = embed_steps(timesteps).astype(BF16)
    hidden = jax.nn.silu(jnp.dot(embedded, time_first, preferred_element_type=F32)).astype(BF16)
    shift = jnp.dot(hidden, time_second, preferred_element_type=F32)
    high = lax.reduce_precision(shift, 8, 7)
    split = jnp.stack([high, shift - high]).reshape(2, 4, 5, 64)
    split = jnp.transpose(split, (2, 1, 0, 3)).reshape(20, 128).astype(BF16)
    split = jnp.pad(split, ((0, 12), (0, 0)))
    rows = jnp.concatenate([below, narrow, above, jnp.zeros_like(narrow[:, :, :1])], axis=2)
    rows = jnp.transpose(rows.reshape(2, 2, 40, 64), (0, 2, 1, 3)).reshape(80, 128)
    slab = jnp.concatenate([rows, split], axis=0)
    slabs = [slab] + [from_partner(slab, k) for k in (1, 2, 3)]
    win = jnp.transpose(inlet_weight.reshape(3, 3, 4, C), (3, 1, 2, 0))
    win = jnp.pad(win, ((0, 0), (0, 0), (0, 0), (0, 7))).reshape(C, 120)
    win = jnp.pad(win, ((0, 0), (0, 8)))
    wres = res_weight.reshape(9 * C, C).T
    wqkv = jnp.concatenate([query_weight, key_weight, value_weight], axis=1).T
    wo = output_weight.T
    wout = jnp.transpose(outlet_weight.reshape(3, 3, C, 4), (0, 1, 3, 2)).reshape(3, 12, C)
    wout = jnp.pad(wout, ((0, 0), (0, 4), (0, 0))).reshape(48, C)
    sent = core(slabs, win, wres, wqkv, wo, wout)
    total = sent[0].astype(F32)
    for k in (1, 2, 3):
        total = total + from_partner(sent[k], k).astype(F32)
    total = total.reshape(2, 4, 8, 128)
    from_below = from_row(total[:, :, 6], 1)
    from_above = from_row(total[:, :, 0], -1)
    middle = total[:, :, 1:6]
    middle = middle + jnp.pad(
        from_below[:, :, None], ((0, 0), (0, 0), (0, 4), (0, 0))
    ) + jnp.pad(from_above[:, :, None], ((0, 0), (0, 0), (4, 0), (0, 0)))
    predicted = jnp.transpose(middle.reshape(2, 4, 5, 2, 64), (0, 3, 1, 2, 4)).reshape(4, 4, 5, 64)

    def per_slot(i):
        return step_coefs[i][:, None, None, None]

    stepped = per_slot(0) * latent + per_slot(1) * predicted + per_slot(2) * step_noise[0]
    count = lax.axis_size("chain")
    arrived = lax.ppermute(stepped[:1], "chain", [(i + 1, i) for i in range(count - 1)])
    is_last = lax.axis_index("chain") == count - 1
    tail = jnp.where(is_last, fresh_noise, arrived)
    advanced = jnp.concatenate([stepped[1:], tail], axis=0)
    return stepped[None], advanced[None]


def solution(mesh):
    rows = P(None, "chain", None, "mp", None)
    return jax.shard_map(
        local,
        mesh=mesh,
        in_specs=(rows, rows, P(None, None, "mp", None), P("chain"), P(None, "chain"))
        + (P(),) * 9,
        out_specs=(rows, rows),
        check_vma=False,
    )
```

time: 226 us -> 70.2 us (0.31)
  the two profiles are of different devices: /device:TPU:231 before, /device:TPU:24 now
where the time goes in v1:
time: 70.2 us; the launch traced here: 69.5 us
  starting transfers between devices  24 us (34%)
  Pallas kernels  20.8 us (30%)
  local copies, waits for them, and re-layouts  9.84 us (14%)
  waiting for transfers between devices  8.71 us (12%)
  other arithmetic  3.51 us (5%)
  matrix products  1.68 us (2%)
  between operations  1.01 us (1%)
    pallas_call x1, Pallas kernels, core(): pl.pallas_call(core_kernel, out_shape=(out,) * 4, in_specs=[vmem] * 9, ou...  20.8 us
    ppermute x4, starting transfers between devices, from_row(): return lax.ppermute(block, 'mp', pairs)  14 us
    ppermute x1, starting transfers between devices, local(): lax.ppermute(stepped[:1], 'chain', [(i + 1, i) for i in range(count - 1)])  5.85 us
    ppermute x4, waiting for transfers between devices, from_row(): return lax.ppermute(block, 'mp', pairs)  5.64 us
    unnamed x27, local copies, waits for them, and re-layouts  5.35 us
    ppermute x6, starting transfers between devices, from_partner(): return lax.ppermute(block, 'chain', [(i, i ^ bits) for i in range(count)])  4.15 us
    ppermute x6, waiting for transfers between devices, from_partner(): return lax.ppermute(block, 'chain', [(i, i ^ bits) for i in range(count)])  3.07 us
    reshape x1, local copies, waits for them, and re-layouts, local(): wres = res_weight.reshape(9 * C, C).T  2.97 us
  transfers between devices with their start and end apart: 11, of which 3 were waited for; matrix products, arithmetic and copies ran while one was open for 14% of the time, Pallas kernels for 0%

profile of v1, /device:TPU:24, one launch (start us, length us, event | category | flops | bytes accessed | tf_op | source)
XLA Modules:
  0.0 69.5 jit_solution(6055531268256745165)
XLA Ops:
  0.6 0.0 copy-start
  0.6 0.0 copy-start.3
  0.7 0.0 copy-start.4
  0.7 0.0 copy-start.5
  0.7 0.9 %copy.58 = bf16[1,4,4,5,64]{4,2,1,3,0:T(4,128)(2,1)S(1)} copy(f32[1,4,4,5,64]{4,2,3,1,0:T(4,128)} %param.14) | data formatting | bytes 30720 | tf_op args[0]
  1.6 3.4 %collective-permute-start = (bf16[4,4,2,64]{3,1,0,2:T(4,128)(2,1)S(1)}, bf16[4,4,2,64]{3,1,0,2:T(4,128)(2,1)S(1)}, u32[]{:S(2)}, u32[]{:S(2)}) collective-permute-start(bf16[4,4,2,64]{3,1,0,2:T(4,128)(2,1)S(1)} %get-tuple-element.16), channel_id=1, source_target_pairs={{0,1},{1,2},{2,3},{3,4},{4,5},{5,6},{6,7},{8,9},{9,10},{10,11},{11... | collective-permute-start | bytes 12296 | tf_op jit(solution)/shard_map/ppermute | solution.py:27
  5.0 4.6 %collective-permute-start.1 = (bf16[4,4,2,64]{3,1,0,2:T(4,128)(2,1)S(1)}, bf16[4,4,2,64]{3,1,0,2:T(4,128)(2,1)S(1)}, u32[]{:S(2)}, u32[]{:S(2)}) collective-permute-start(bf16[4,4,2,64]{3,1,0,2:T(4,128)(2,1)S(1)} %get-tuple-element.17), channel_id=1, source_target_pairs={{1,0},{2,1},{3,2},{4,3},{5,4},{6,5},{7,6},{9,8},{10,9},{11,10},{12... | collective-permute-start | bytes 12296 | tf_op jit(solution)/shard_map/ppermute | solution.py:27
  9.6 0.7 convert_element_type.42
  10.2 0.1 fusion.10
  10.4 0.0 copy-done
  10.4 1.7 %reduce-precision_convert_fusion = (bf16[4,320]{1,0:T(4,128)(2,1)S(1)}, bf16[4,320]{1,0:T(4,128)(2,1)S(1)}) fusion(bf16[1280,320]{0,1:T(8,128)(2,1)S(1)} %copy-done, bf16[320,1280]{1,0:T(8,128)(2,1)} %param.20, bf16[4,160]{1,0:T(4,128)(2,1)S(1)} %get-tuple-element.24, bf16[4,160]{1,0:T(4,128)(2,1)S(1)} %get-tuple-element.23), kind=kOutput, calls=%fused_computation.24 | convolution fusion | flops 6589440 | bytes 1646080 | tf_op jit(solution)/shard_map/dot_general | solution.py:220
  12.0 0.1 stack.9
  12.2 0.1 stack.10
  12.3 0.1 convert_element_type.45
  12.4 0.0 copy-done.3
  12.4 0.2 copy.34
  12.6 0.0 copy-done.4
  12.6 0.0 copy-start.7
  12.6 0.0 copy-start.8
  12.6 0.2 copy.35
  12.8 0.0 copy-done.5
  12.8 0.2 copy.36
  13.0 0.0 copy-start.6
  13.0 0.1 pad.46.clone
  13.1 0.0 collective-permute-done
  13.1 0.0 collective-permute-done.1
  13.1 0.1 maximum_maximum_fusion
  13.3 0.1 reshape.66
  13.4 0.9 %collective-permute-start.4 = (bf16[112,128]{1,0:T(8,128)(2,1)S(1)}, bf16[112,128]{1,0:T(8,128)(2,1)}, u32[]{:S(2)}, u32[]{:S(2)}) collective-permute-start(bf16[112,128]{1,0:T(8,128)(2,1)S(1)} %fusion.3.s0), channel_id=1, source_target_pairs={{0,24},{8,16},{16,8},{24,0},{32,56},{40,48},{48,40},{56,32},{64,88... | collective-permute-start | bytes 86024 | tf_op jit(solution)/shard_map/ppermute | solution.py:21
  14.3 1.2 %collective-permute-start.3 = (bf16[112,128]{1,0:T(8,128)(2,1)S(1)}, bf16[112,128]{1,0:T(8,128)(2,1)}, u32[]{:S(2)}, u32[]{:S(2)}) collective-permute-start(bf16[112,128]{1,0:T(8,128)(2,1)S(1)} %fusion.3.s0), channel_id=1, source_target_pairs={{0,16},{8,24},{16,0},{24,8},{32,48},{40,56},{48,32},{56,40},{64,80... | collective-permute-start | bytes 86024 | tf_op jit(solution)/shard_map/ppermute | solution.py:21
  15.5 0.0 collective-permute-start.2
  15.5 0.1 maximum_bitcast_fusion.wqkv
  15.6 0.0 copy-done.7
  15.6 0.0 copy-done.8
  15.7 0.6 pad.27
  16.3 0.1 reshape.68
  16.4 0.1 copy.32
  16.5 0.0 copy-done.6
  16.5 0.9 %copy.37 = bf16[320,320]{0,1:T(8,128)(2,1)} copy(bf16[320,320]{1,0:T(8,128)(2,1)S(1)} %copy-done.6) | data formatting | bytes 409600 | tf_op args[12]
  17.4 3.0 %copy.33 = bf16[2880,320]{0,1:T(8,128)(2,1)S(1)} copy(bf16[2880,320]{1,0:T(8,128)(2,1)} %bitcast.59) | data formatting | bytes 3686400 | tf_op jit(solution)/shard_map/reshape | solution.py:232
  20.4 0.0 collective-permute-done.4.s3
  20.4 0.0 collective-permute-done.3.s2
  20.4 0.0 collective-permute-done.2.s1
  20.4 0.9 %copy-done.1 = bf16[320,320]{0,1:T(8,128)(2,1)S(1)} copy-done((bf16[320,320]{0,1:T(8,128)(2,1)S(1)}, bf16[320,320]{0,1:T(8,128)(2,1)}, u32[]{:S(2)}) %copy-start.1) | copy-done | bytes 204824
  21.4 0.8 %copy-done.2 = bf16[3,16,320]{2,1,0:T(8,128)(2,1)S(1)} copy-done((bf16[3,16,320]{2,1,0:T(8,128)(2,1)S(1)}, bf16[3,16,320]{2,1,0:T(8,128)(2,1)}, u32[]{:S(2)}) %copy-start.2) | copy-done | bytes 30744
  22.1 20.8 %shard_map.149 = (bf16[64,128]{1,0:T(8,128)(2,1)S(1)}, bf16[64,128]{1,0:T(8,128)(2,1)S(1)}, bf16[64,128]{1,0:T(8,128)(2,1)S(1)}, bf16[64,128]{1,0:T(8,128)(2,1)S(1)}) custom-call(bf16[112,128]{1,0:T(8,128)(2,1)S(1)} %fusion.3.s0, bf16[112,128]{1,0:T(8,128)(2,1)} %collective-permute-done.2.s1, bf16[112,128]{1,0:T(8,128)(2,1)} %collective-permute-done.3.s2, ...), custom_call_target="tpu_custom_call" | custom-call | flops 4000000000 | bytes 3000000 | tf_op jit(solution)/shard_map/pallas_call | solution.py:181
  42.9 0.6 collective-permute-start.5
  43.5 1.4 %collective-permute-start.6 = (bf16[64,128]{1,0:T(8,128)(2,1)S(1)}, bf16[64,128]{1,0:T(8,128)(2,1)S(1)}, u32[]{:S(2)}, u32[]{:S(2)}) collective-permute-start(bf16[64,128]{1,0:T(8,128)(2,1)S(1)} %get-tuple-element.8), channel_id=1, source_target_pairs={{0,16},{8,24},{16,0},{24,8},{32,48},{40,56},{48,32},{56,40},{64,80... | collective-permute-start | bytes 49160 | tf_op jit(solution)/shard_map/ppermute | solution.py:21
  44.8 0.1 collective-permute-start.7
  44.9 0.0 collective-permute-done.5
  44.9 2.3 %collective-permute-done.6 = bf16[64,128]{1,0:T(8,128)(2,1)S(1)} collective-permute-done((bf16[64,128]{1,0:T(8,128)(2,1)S(1)}, bf16[64,128]{1,0:T(8,128)(2,1)S(1)}, u32[]{:S(2)}, u32[]{:S(2)}) %collective-permute-start.6) | collective-permute-done | bytes 16416 | tf_op jit(solution)/shard_map/ppermute | solution.py:21
  47.2 0.8 %collective-permute-done.7 = bf16[64,128]{1,0:T(8,128)(2,1)S(1)} collective-permute-done((bf16[64,128]{1,0:T(8,128)(2,1)S(1)}, bf16[64,128]{1,0:T(8,128)(2,1)S(1)}, u32[]{:S(2)}, u32[]{:S(2)}) %collective-permute-start.7) | collective-permute-done | bytes 16416 | tf_op jit(solution)/shard_map/ppermute | solution.py:21
  48.0 4.1 %collective-permute-start.9 = (f32[2,4,128]{2,1,0:T(4,128)S(1)}, f32[2,4,128]{2,1,0:T(4,128)S(1)}, u32[]{:S(2)}, u32[]{:S(2)}) collective-permute-start(f32[2,4,128]{2,1,0:T(4,128)S(1)} %bitcast.71), channel_id=1, source_target_pairs={{1,0},{2,1},{3,2},{4,3},{5,4},{6,5},{7,6},{9,8},{10,9},{11,10},{12... | collective-permute-start | bytes 12296 | tf_op jit(solution)/shard_map/ppermute | solution.py:27
  52.1 1.9 %collective-permute-start.8 = (f32[2,4,128]{2,1,0:T(4,128)S(1)}, f32[2,4,128]{2,1,0:T(4,128)S(1)}, u32[]{:S(2)}, u32[]{:S(2)}) collective-permute-start(f32[2,4,128]{2,1,0:T(4,128)S(1)} %bitcast.70), channel_id=1, source_target_pairs={{0,1},{1,2},{2,3},{3,4},{4,5},{5,6},{6,7},{8,9},{9,10},{10,11},{11... | collective-permute-start | bytes 12296 | tf_op jit(solution)/shard_map/ppermute | solution.py:27
  54.1 0.0 collective-permute-done.9
  54.1 5.6 %collective-permute-done.8 = f32[2,4,128]{2,1,0:T(4,128)S(1)} collective-permute-done((f32[2,4,128]{2,1,0:T(4,128)S(1)}, f32[2,4,128]{2,1,0:T(4,128)S(1)}, u32[]{:S(2)}, u32[]{:S(2)}) %collective-permute-start.8) | collective-permute-done | bytes 4128 | tf_op jit(solution)/shard_map/ppermute | solution.py:27
  59.8 0.1 fusion.26
  59.9 0.9 %fusion.1 = f32[4,4,5,64]{3,1,0,2:T(4,128)S(1)} fusion(f32[4,4,5,64]{3,1,0,2:T(4,128)S(1)} %bitcast.60, f32[1,4,4,5,64]{4,2,3,1,0:T(4,128)} %param.15, f32[1,4,4,5,64]{4,2,3,1,0:T(4,128)} %param.14, f32[4]{0:T(128)S(1)} %get-tuple-element.21, f32[4]{0:T(128)S(1)} %get-tuple-element.22, f32[4]{0:T(128)S(1)} %get-tuple-element.20), kind=kLoop, calls=%fused_computation.7 | loop fusion | flops 25600 | bytes 81968 | tf_op jit(solution)/shard_map/add | solution.py:253
  60.8 5.8 %collective-permute-start.10 = (f32[1,4,5,64]{3,1,0,2:T(4,128)S(1)}, f32[1,4,5,64]{3,1,0,2:T(4,128)S(1)}, u32[]{:S(2)}, u32[]{:S(2)}) collective-permute-start(f32[1,4,5,64]{3,1,0,2:T(4,128)S(1)} %slice.56), channel_id=1, source_target_pairs={{8,0},{16,8},{24,16},{32,24},{40,32},{48,40},{56,48},{64,56},{72,6... | collective-permute-start | bytes 15368 | tf_op jit(solution)/shard_map/ppermute | solution.py:255
  66.6 0.9 %multiply_add_fusion = f32[1,4,4,5,64]{4,2,1,3,0:T(4,128)S(1)} fusion(f32[1,4,4,5,64]{4,2,1,3,0:T(4,128)S(1)} %bitcast.61, f32[1,4,4,5,64]{4,2,3,1,0:T(4,128)} %param.15, f32[1,4,4,5,64]{4,2,3,1,0:T(4,128)} %param.14, f32[4]{0:T(128)S(1)} %get-tuple-element.21, f32[4]{0:T(128)S(1)} %get-tuple-element.22, f32[4]{0:T(128)S(1)} %get-tuple-element.20), kind=kLoop, calls=%fused_computation.11 | loop fusion | flops 25600 | bytes 81968 | tf_op jit(solution)/shard_map/add | solution.py:253
  67.5 0.6 copy.44
  68.1 0.0 collective-permute-done.10
  68.1 0.7 %bitcast_select_fusion = f32[1,4,5,64]{3,1,0,2:T(4,128)S(1)} fusion(f32[1,4,5,64]{3,1,0,2:T(4,128)S(1)} %collective-permute-done.10, f32[1,4,5,64]{3,1,2,0:T(4,128)} %param.16, pred[]{:T(512)S(6)} %eq.3), kind=kLoop, calls=%fused_computation.21 | loop fusion | flops 1280 | bytes 15361 | tf_op jit(solution)/shard_map/jit(_where)/select_n | solution.py:257
  68.9 0.6 copy.45
  (24 shorter events, 0.3 us)
Async XLA Ops:
  0.6 9.7 %copy-start = (bf16[1280,320]{0,1:T(8,128)(2,1)S(1)}, bf16[1280,320]{0,1:T(8,128)(2,1)}, u32[]{:S(2)}) copy-start(bf16[1280,320]{0,1:T(8,128)(2,1)} %param.21) | copy-start | bytes 2457604
  0.6 11.7 %copy-start.3 = (bf16[320,320]{1,0:T(8,128)(2,1)S(1)}, bf16[320,320]{1,0:T(8,128)(2,1)}, u32[]{:S(2)}) copy-start(bf16[320,320]{1,0:T(8,128)(2,1)} %param.23) | copy-start | bytes 614404
  0.7 11.9 %copy-start.4 = (bf16[320,320]{1,0:T(8,128)(2,1)S(1)}, bf16[320,320]{1,0:T(8,128)(2,1)}, u32[]{:S(2)}) copy-start(bf16[320,320]{1,0:T(8,128)(2,1)} %param.24) | copy-start | bytes 614404
  0.7 12.1 %copy-start.5 = (bf16[320,320]{1,0:T(8,128)(2,1)S(1)}, bf16[320,320]{1,0:T(8,128)(2,1)}, u32[]{:S(2)}) copy-start(bf16[320,320]{1,0:T(8,128)(2,1)} %param.25) | copy-start | bytes 614404
  1.6 11.5 %collective-permute-start = (bf16[4,4,2,64]{3,1,0,2:T(4,128)(2,1)S(1)}, bf16[4,4,2,64]{3,1,0,2:T(4,128)(2,1)S(1)}, u32[]{:S(2)}, u32[]{:S(2)}) collective-permute-start(bf16[4,4,2,64]{3,1,0,2:T(4,128)(2,1)S(1)} %get-tuple-element.16), channel_id=1, source_target_pairs={{0,1},{1,2},{2,3},{3,4},{4,5},{5,6},{6,7},{8,9},{9,10},{10,11},{11... | collective-permute-start | bytes 12296 | tf_op jit(solution)/shard_map/ppermute | solution.py:27
  5.0 8.1 %collective-permute-start.1 = (bf16[4,4,2,64]{3,1,0,2:T(4,128)(2,1)S(1)}, bf16[4,4,2,64]{3,1,0,2:T(4,128)(2,1)S(1)}, u32[]{:S(2)}, u32[]{:S(2)}) collective-permute-start(bf16[4,4,2,64]{3,1,0,2:T(4,128)(2,1)S(1)} %get-tuple-element.17), channel_id=1, source_target_pairs={{1,0},{2,1},{3,2},{4,3},{5,4},{6,5},{7,6},{9,8},{10,9},{11,10},{12... | collective-permute-start | bytes 12296 | tf_op jit(solution)/shard_map/ppermute | solution.py:27
  12.6 3.0 %copy-start.7 = (bf16[9,4,320]{2,1,0:T(4,128)(2,1)S(1)}, bf16[9,4,320]{2,1,0:T(4,128)(2,1)}, u32[]{:S(2)}) copy-start(bf16[9,4,320]{2,1,0:T(4,128)(2,1)} %param.19) | copy-start | bytes 69124
  12.6 3.0 %copy-start.8 = (bf16[9,320,4]{1,2,0:T(4,128)(2,1)S(1)}, bf16[9,320,4]{1,2,0:T(4,128)(2,1)}, u32[]{:S(2)}) copy-start(bf16[9,320,4]{1,2,0:T(4,128)(2,1)} %param.27) | copy-start | bytes 69124
  13.0 3.5 %copy-start.6 = (bf16[320,320]{1,0:T(8,128)(2,1)S(1)}, bf16[320,320]{1,0:T(8,128)(2,1)}, u32[]{:S(2)}) copy-start(bf16[320,320]{1,0:T(8,128)(2,1)} %param.26) | copy-start | bytes 614404
  13.4 7.0 %collective-permute-start.4 = (bf16[112,128]{1,0:T(8,128)(2,1)S(1)}, bf16[112,128]{1,0:T(8,128)(2,1)}, u32[]{:S(2)}, u32[]{:S(2)}) collective-permute-start(bf16[112,128]{1,0:T(8,128)(2,1)S(1)} %fusion.3.s0), channel_id=1, source_target_pairs={{0,24},{8,16},{16,8},{24,0},{32,56},{40,48},{48,40},{56,32},{64,88... | collective-permute-start | bytes 86024 | tf_op jit(solution)/shard_map/ppermute | solution.py:21
  14.3 6.1 %collective-permute-start.3 = (bf16[112,128]{1,0:T(8,128)(2,1)S(1)}, bf16[112,128]{1,0:T(8,128)(2,1)}, u32[]{:S(2)}, u32[]{:S(2)}) collective-permute-start(bf16[112,128]{1,0:T(8,128)(2,1)S(1)} %fusion.3.s0), channel_id=1, source_target_pairs={{0,16},{8,24},{16,0},{24,8},{32,48},{40,56},{48,32},{56,40},{64,80... | collective-permute-start | bytes 86024 | tf_op jit(solution)/shard_map/ppermute | solution.py:21
  15.5 4.9 %collective-permute-start.2 = (bf16[112,128]{1,0:T(8,128)(2,1)S(1)}, bf16[112,128]{1,0:T(8,128)(2,1)}, u32[]{:S(2)}, u32[]{:S(2)}) collective-permute-start(bf16[112,128]{1,0:T(8,128)(2,1)S(1)} %fusion.3.s0), channel_id=1, source_target_pairs={{0,8},{8,0},{16,24},{24,16},{32,40},{40,32},{48,56},{56,48},{64,72... | collective-permute-start | bytes 86024 | tf_op jit(solution)/shard_map/ppermute | solution.py:21
  20.4 0.9 %copy-start.1 = (bf16[320,320]{0,1:T(8,128)(2,1)S(1)}, bf16[320,320]{0,1:T(8,128)(2,1)}, u32[]{:S(2)}) copy-start(bf16[320,320]{0,1:T(8,128)(2,1)} %copy.37) | copy-start | bytes 614404
  21.3 0.8 %copy-start.2 = (bf16[3,16,320]{2,1,0:T(8,128)(2,1)S(1)}, bf16[3,16,320]{2,1,0:T(8,128)(2,1)}, u32[]{:S(2)}) copy-start(bf16[3,16,320]{2,1,0:T(8,128)(2,1)} %pad.27) | copy-start | bytes 92164
  22.1 31.9 %copy-start.9 = (f32[3,4]{1,0:T(4,128)S(1)}, f32[3,4]{1,0:T(4,128)}, u32[]{:S(2)}) copy-start(f32[3,4]{1,0:T(4,128)} %param.18) | copy-start | bytes 148
  42.9 2.0 %collective-permute-start.5 = (bf16[64,128]{1,0:T(8,128)(2,1)S(1)}, bf16[64,128]{1,0:T(8,128)(2,1)S(1)}, u32[]{:S(2)}, u32[]{:S(2)}) collective-permute-start(bf16[64,128]{1,0:T(8,128)(2,1)S(1)} %get-tuple-element.7), channel_id=1, source_target_pairs={{0,8},{8,0},{16,24},{24,16},{32,40},{40,32},{48,56},{56,48},{64,72... | collective-permute-start | bytes 49160 | tf_op jit(solution)/shard_map/ppermute | solution.py:21
  43.5 3.7 %collective-permute-start.6 = (bf16[64,128]{1,0:T(8,128)(2,1)S(1)}, bf16[64,128]{1,0:T(8,128)(2,1)S(1)}, u32[]{:S(2)}, u32[]{:S(2)}) collective-permute-start(bf16[64,128]{1,0:T(8,128)(2,1)S(1)} %get-tuple-element.8), channel_id=1, source_target_pairs={{0,16},{8,24},{16,0},{24,8},{32,48},{40,56},{48,32},{56,40},{64,80... | collective-permute-start | bytes 49160 | tf_op jit(solution)/shard_map/ppermute | solution.py:21
  44.8 3.2 %collective-permute-start.7 = (bf16[64,128]{1,0:T(8,128)(2,1)S(1)}, bf16[64,128]{1,0:T(8,128)(2,1)S(1)}, u32[]{:S(2)}, u32[]{:S(2)}) collective-permute-start(bf16[64,128]{1,0:T(8,128)(2,1)S(1)} %get-tuple-element.9), channel_id=1, source_target_pairs={{0,24},{8,16},{16,8},{24,0},{32,56},{40,48},{48,40},{56,32},{64,88... | collective-permute-start | bytes 49160 | tf_op jit(solution)/shard_map/ppermute | solution.py:21
  48.0 6.1 %collective-permute-start.9 = (f32[2,4,128]{2,1,0:T(4,128)S(1)}, f32[2,4,128]{2,1,0:T(4,128)S(1)}, u32[]{:S(2)}, u32[]{:S(2)}) collective-permute-start(f32[2,4,128]{2,1,0:T(4,128)S(1)} %bitcast.71), channel_id=1, source_target_pairs={{1,0},{2,1},{3,2},{4,3},{5,4},{6,5},{7,6},{9,8},{10,9},{11,10},{12... | collective-permute-start | bytes 12296 | tf_op jit(solution)/shard_map/ppermute | solution.py:27
  52.1 7.6 %collective-permute-start.8 = (f32[2,4,128]{2,1,0:T(4,128)S(1)}, f32[2,4,128]{2,1,0:T(4,128)S(1)}, u32[]{:S(2)}, u32[]{:S(2)}) collective-permute-start(f32[2,4,128]{2,1,0:T(4,128)S(1)} %bitcast.70), channel_id=1, source_target_pairs={{0,1},{1,2},{2,3},{3,4},{4,5},{5,6},{6,7},{8,9},{9,10},{10,11},{11... | collective-permute-start | bytes 12296 | tf_op jit(solution)/shard_map/ppermute | solution.py:27
  60.8 7.4 %collective-permute-start.10 = (f32[1,4,5,64]{3,1,0,2:T(4,128)S(1)}, f32[1,4,5,64]{3,1,0,2:T(4,128)S(1)}, u32[]{:S(2)}, u32[]{:S(2)}) collective-permute-start(f32[1,4,5,64]{3,1,0,2:T(4,128)S(1)} %slice.56), channel_id=1, source_target_pairs={{8,0},{16,8},{24,16},{32,24},{40,32},{48,40},{56,48},{64,56},{72,6... | collective-permute-start | bytes 15368 | tf_op jit(solution)/shard_map/ppermute | solution.py:255

commit v2 on v1

v2 whole, which is shorter than its diff:
```python
import functools
import math

import jax
import jax.numpy as jnp
from jax import lax
from jax.experimental import pallas as pl
from jax.experimental.pallas import tpu as pltpu
from jax.sharding import PartitionSpec as P

F32 = jnp.float32
BF16 = jnp.bfloat16
HEADS = 5
HEAD_DIM = 64
C = 320
ROWS = 5
GROUP = 4


def from_partner(block, bits):
    count = lax.axis_size("chain")
    return lax.ppermute(block, "chain", [(i, i ^ bits) for i in range(count)])


def from_row(block, by):
    count = lax.axis_size("mp")
    return lax.ppermute(block, "mp", [(i, (i + by) % count) for i in range(count)])


def embed_steps(timesteps):
    half_dim = C // 2
    frequency = jnp.exp(-math.log(10000.0) * jnp.arange(half_dim, dtype=F32) / half_dim)
    angles = timesteps.astype(F32)[:, None] * frequency[None, :]
    return jnp.concatenate([jnp.cos(angles), jnp.sin(angles)], axis=1)


def halved_silu(half):
    return half * jnp.tanh(half) + half


def inv_rms(values):
    return lax.rsqrt(jnp.sum(values * values, axis=0, keepdims=True) * (1.0 / C) + 1e-05)


def iota(shape, dim):
    return lax.broadcasted_iota(jnp.int32, shape, dim)


def mm(a, b):
    return jnp.dot(a, b, preferred_element_type=F32)


def prep_kernel(inlet, wres, outlet, win_t, wres_t, wout_t, rows):
    rows[...] = jnp.zeros_like(rows)
    for dy in range(3):
        for dx in range(3):
            at = 32 * dx + 4 * dy
            rows[at : at + 4, :] = inlet[3 * dy + dx].astype(F32)
    taps = rows[...].T
    for r in range(6):
        win_t[r] = (taps if r == 0 else pltpu.roll(taps, 4 * r, 1)).astype(BF16)
    for at in range(0, 9 * C, 128):
        size = min(128, 9 * C - at)
        wres_t[:, at : at + size] = wres[at : at + size, :].T
    for a in range(3):
        for b in range(3):
            at = 16 * a + 4 * b
            rows[at : at + 4, :] = outlet[3 * a + b].astype(F32)
        rows[16 * a + 12 : 16 * a + 16, :] = jnp.zeros((4, C), F32)
    wout_t[...] = rows[:48, :].astype(BF16)


def prep(inlet, wres, outlet):
    vmem = pl.BlockSpec(memory_space=pltpu.VMEM)
    shapes = ((6, C, 128), (C, 9 * C), (48, C))
    return pl.pallas_call(
        prep_kernel,
        out_shape=tuple(jax.ShapeDtypeStruct(s, BF16) for s in shapes),
        in_specs=[vmem] * 3,
        out_specs=(vmem,) * 3,
        scratch_shapes=[pltpu.VMEM((128, C), F32)],
        compiler_params=pltpu.CompilerParams(vmem_limit_bytes=32 * 1024 * 1024),
        cost_estimate=pl.CostEstimate(
            flops=2_000_000_000, bytes_accessed=6_000_000, transcendentals=0
        ),
    )(inlet, wres, outlet)


def core_kernel(
    s0, s1, s2, s3, win, wres, wq, wk, wv, wo_in, wout,
    o0, o1, o2, o3,
    opn, act, res, nrm, qkv, scr, att, accs, wqkv, wo,
):
    tile = lax.axis_index("chain") % GROUP
    row_block = lax.axis_index("mp")
    last_row = lax.axis_size("mp") - 1
    slabs = [s0[...], s1[...], s2[...], s3[...]]
    shift_rows = jnp.concatenate([s[96:128] for s in slabs], axis=0)
    er, el = iota((128, 640), 0), iota((128, 640), 1)
    pick = (er % 32 // 4 == el // 128) & (er // 32 * 4 + er % 4 == el % 128 // 8)
    spread = mm(shift_rows.astype(F32).T.astype(BF16), pick.astype(F32).astype(BF16))
    spread = spread[:64] + spread[64:]
    shift = jnp.concatenate([spread[:, 128 * i : 128 * i + 128] for i in range(5)], axis=0) * 0.5
    latent = jnp.concatenate([s[:96] for s in slabs], axis=0)
    lane = iota((128, 384), 1)
    cell, slot, block = lane % 8, lane % 128 // 8, lane // 128
    at = jnp.where(
        block < 2,
        16 * tile + 8 * block + cell,
        jnp.where(cell == 0, 16 * tile - 1, jnp.where(cell == 7, 16 * tile + 16, -1000)),
    )
    src = iota((128, 384), 0)
    same_half = src // 64 == slot % 2
    pair_of = iota((1, 1, 384), 2) % 128 // 16
    pair_no = iota((8, 1, 384), 0)
    row_of = iota((48, 384), 0) // 4
    inside = ((row_block > 0) | (row_of >= 3)) & ((row_block < last_row) | (row_of < 3 + ROWS))
    columns = []
    for dx in range(3):
        chosen = same_half & (src % 64 == at + (dx - 1))
        moved = mm(latent, chosen.astype(F32).astype(BF16))
        moved = jnp.where(pair_of == pair_no, moved.reshape(8, 48, 384), 0.0)
        columns.append(jnp.where(inside, jnp.sum(moved, axis=0), 0.0))
    empty = jnp.zeros((32, 384), F32)
    upper = jnp.concatenate([c[:32] for c in columns] + [empty], axis=0).astype(BF16)
    lower = jnp.concatenate([c[16:] for c in columns] + [empty], axis=0).astype(BF16)

    lane1 = iota((1, 128), 1)
    cell1 = lane1 % 8
    first, last = cell1 == 0, cell1 == 7
    side = jnp.where(
        first & (tile > 0), 1.0, jnp.where(last & (tile < GROUP - 1), 1.0, 0.0)
    )
    same_cell = iota((8, 128), 0) == iota((8, 128), 1) % 8
    log2e8 = math.log2(math.e) / math.sqrt(HEAD_DIM)

    def open_row(r):
        opn[r] = mm(win[r], upper) if r < 6 else mm(win[r - 4], lower)

    def activate(r):
        opening = opn[r]
        scale = inv_rms(opening) * 0.5
        parts = []
        for t in range(3):
            piece = slice(128 * t, 128 * t + 128)
            part = halved_silu(opening[:, piece] * scale[:, piece] + shift)
            if t == 2:
                part = part * side
            if r < 2:
                part = part * jnp.where(row_block > 0, 1.0, 0.0)
            if r > ROWS + 1:
                part = part * jnp.where(row_block < last_row, 1.0, 0.0)
            parts.append(part)
        a0, a1, edge = parts
        base = 960 * r
        act[base : base + 320, :128] = jnp.where(first, edge, pltpu.roll(a0, 1, 1)).astype(BF16)
        act[base : base + 320, 128:] = jnp.where(
            first, pltpu.roll(a0, 121, 1), pltpu.roll(a1, 1, 1)
        ).astype(BF16)
        act[base + 320 : base + 640, :128] = a0.astype(BF16)
        act[base + 320 : base + 640, 128:] = a1.astype(BF16)
        act[base + 640 : base + 960, :128] = jnp.where(
            last, pltpu.roll(a1, 7, 1), pltpu.roll(a0, 127, 1)
        ).astype(BF16)
        act[base + 640 : base + 960, 128:] = jnp.where(
            last, edge, pltpu.roll(a1, 127, 1)
        ).astype(BF16)

    def convolve(r):
        residual = opn[r + 1, :, :256] + mm(wres[...], act[960 * r : 960 * r + 2880, :])
        res[r] = residual
        nrm[r] = (residual * inv_rms(residual)).astype(BF16)

    def project(r):
        qkv[r] = mm(wqkv[...], nrm[r]).astype(BF16)

    def score(r):
        for b in range(2):
            piece = slice(128 * b, 128 * b + 128)
            for h in range(HEADS):
                scr[r % 2, HEADS * b + h] = lax.dot_general(
                    qkv[r, 320 + 64 * h : 384 + 64 * h, piece],
                    qkv[r, 64 * h : 64 * h + 64, piece],
                    (((0,), (0,)), ((), ())),
                    preferred_element_type=F32,
                ).reshape(16, 8, 128)

    def attend(r):
        probs = []
        for i in range(2 * HEADS):
            scores = scr[r % 2, i]
            highest = jnp.max(scores, axis=0)
            expd = jnp.exp2((scores - highest) * log2e8)
            share = jnp.where(same_cell, 1.0 / jnp.sum(expd, axis=0), 0.0)
            probs.append((expd * share).reshape(128, 128).astype(BF16))
        for b in range(2):
            piece = slice(128 * b, 128 * b + 128)
            for h in range(HEADS):
                value = qkv[r, 640 + 64 * h : 704 + 64 * h, piece]
                att[r, 64 * h : 64 * h + 64, piece] = mm(value, probs[HEADS * b + h]).astype(BF16)

    def mix(r):
        mixture = res[r] + mm(wo[...], att[r])
        outer = halved_silu(mixture * (0.5 * inv_rms(mixture)))
        if r == 0:
            outer = outer * jnp.where(row_block > 0, 1.0, 0.0)
        if r == ROWS + 1:
            outer = outer * jnp.where(row_block < last_row, 1.0, 0.0)
        nrm[r] = outer.astype(BF16)

    def outlet(r):
        taps = mm(wout[...], nrm[r])
        for a in range(3):
            if 0 <= r - a < ROWS:
                accs[r - a] += taps[16 * a : 16 * a + 16]

    accs[...] = jnp.zeros_like(accs)
    for i, w in enumerate((wq, wk, wv)):
        wqkv[C * i : C * i + C, :] = w[...].T
    wo[...] = wo_in[...].T
    count = ROWS + 2
    for r in range(count + 2):
        open_row(r)
    for r in range(3):
        activate(r)
    for step in range(count + 5):
        if step < count:
            convolve(step)
            if step < count - 1:
                activate(step + 3)
        for late, stage in enumerate((project, score, attend, mix, outlet), 1):
            if 0 <= step - late < count:
                stage(step - late)
    src = iota((256, 128), 0)
    dst = iota((256, 128), 1)
    same_half = src % 128 // 8 % 2 == dst // 64
    spot = 16 * tile + src // 128 * 8 + src % 8 - dst % 64
    pair_of = iota((1, 1, 256), 2) % 128 // 16
    pair_no = iota((8, 1, 256), 0)
    total = None
    for b in range(3):
        chosen = (same_half & (spot == b - 1)).astype(F32).astype(BF16)
        part = accs[:, 4 * b : 4 * b + 4, :].reshape(24, 256)
        high = part.astype(BF16).astype(F32)
        for piece in (high, part - high):
            wide = jnp.where(pair_of == pair_no, piece[None], 0.0)
            term = mm(wide.reshape(192, 256).astype(BF16), chosen)
            total = term if total is None else total + term
    for k, out in enumerate((o0, o1, o2, o3)):
        out[...] = total[48 * k : 48 * k + 48].astype(BF16)


def core(slabs, win, wres, wq, wk, wv, wo, wout):
    out = jax.ShapeDtypeStruct((48, 128), BF16)
    vmem = pl.BlockSpec(memory_space=pltpu.VMEM)
    return pl.pallas_call(
        core_kernel,
        out_shape=(out,) * 4,
        in_specs=[vmem] * 11,
        out_specs=(vmem,) * 4,
        scratch_shapes=[
            pltpu.VMEM((ROWS + 4, C, 384), F32),
            pltpu.VMEM(((ROWS + 4) * 960, 256), BF16),
            pltpu.VMEM((ROWS + 2, C, 256), F32),
            pltpu.VMEM((ROWS + 2, C, 256), BF16),
            pltpu.VMEM((ROWS + 2, 3 * C, 256), BF16),
            pltpu.VMEM((2, 10, 16, 8, 128), F32),
            pltpu.VMEM((ROWS + 2, C, 256), BF16),
            pltpu.VMEM((ROWS + 1, 16, 256), F32),
            pltpu.VMEM((3 * C, C), BF16),
            pltpu.VMEM((C, C), BF16),
        ],
        compiler_params=pltpu.CompilerParams(vmem_limit_bytes=36 * 1024 * 1024),
        cost_estimate=pl.CostEstimate(
            flops=4_000_000_000, bytes_accessed=3_000_000, transcendentals=3_000_000
        ),
    )(*slabs, win, wres, wq, wk, wv, wo, wout)


def local(
    latents,
    step_noise,
    fresh_noise,
    timesteps,
    step_coefs,
    inlet_weight,
    time_first,
    time_second,
    res_weight,
    query_weight,
    key_weight,
    value_weight,
    output_weight,
    outlet_weight,
):
    latent = jnp.transpose(latents[0], (0, 2, 1, 3))
    noise = jnp.transpose(step_noise[0], (0, 2, 1, 3))
    fresh = jnp.transpose(fresh_noise, (0, 2, 1, 3))
    below = from_row(latent, 1)[:, ROWS - 3 :]
    above = from_row(latent, -1)[:, :3]
    embedded = embed_steps(timesteps).astype(BF16)
    hidden = jax.nn.silu(jnp.dot(embedded, time_first, preferred_element_type=F32)).astype(BF16)
    shift = jnp.dot(hidden, time_second, preferred_element_type=F32)
    high = lax.reduce_precision(shift, 8, 7)
    split = jnp.stack([high, shift - high]).reshape(2, 4, 5, 64)
    split = jnp.transpose(split, (2, 1, 0, 3)).reshape(20, 128).astype(BF16)
    split = jnp.pad(split, ((0, 12), (0, 0)))
    rows = jnp.concatenate([below, latent, above, jnp.zeros_like(latent[:, :1])], axis=1)
    rows = jnp.transpose(rows.reshape(2, 2, 48, 64), (0, 2, 1, 3)).reshape(96, 128).astype(BF16)
    slab = jnp.concatenate([rows, split], axis=0)
    slabs = [slab] + [from_partner(slab, k) for k in (1, 2, 3)]
    win, wres, wout = prep(
        inlet_weight, res_weight.reshape(9 * C, C), jnp.transpose(outlet_weight, (0, 2, 1))
    )
    squares = (query_weight, key_weight, value_weight, output_weight)
    sent = core(slabs, win, wres, *squares, wout)
    total = sent[0].astype(F32)
    for k in (1, 2, 3):
        total = total + from_partner(sent[k], k).astype(F32)
    middle = total.reshape(2, 6, 4, 128)[:, :ROWS]
    predicted = jnp.transpose(middle.reshape(2, 5, 4, 2, 64), (0, 3, 1, 2, 4)).reshape(4, 5, 4, 64)

    def per_slot(i):
        return step_coefs[i][:, None, None, None]

    stepped = per_slot(0) * latent + per_slot(1) * predicted + per_slot(2) * noise
    count = lax.axis_size("chain")
    arrived = lax.ppermute(stepped[:1], "chain", [(i, (i - 1) % count) for i in range(count)])
    is_last = lax.axis_index("chain") == count - 1
    tail = jnp.where(is_last, fresh, arrived)
    advanced = jnp.concatenate([stepped[1:], tail], axis=0)
    return tuple(jnp.transpose(x, (0, 2, 1, 3))[None] for x in (stepped, advanced))


def solution(mesh):
    rows = P(None, "chain", None, "mp", None)
    return jax.shard_map(
        local,
        mesh=mesh,
        in_specs=(rows, rows, P(None, None, "mp", None), P("chain"), P(None, "chain"))
        + (P(),) * 9,
        out_specs=(rows, rows),
        check_vma=False,
    )
```

time: 70.2 us -> 41 us (0.58)
  the two profiles are of different devices: /device:TPU:24 before, /device:TPU:6 now
where the time goes in v2:
time: 41 us; the launch traced here: 40.7 us
  starting transfers between devices  15.9 us (39%)
  Pallas kernels  12.3 us (30%)
  waiting for transfers between devices  5.91 us (14%)
  other arithmetic  3.38 us (8%)
  matrix products  1.68 us (4%)
  between operations  0.9 us (2%)
  local copies, waits for them, and re-layouts  0.68 us (2%)
    pallas_call x1, Pallas kernels, core(): pl.pallas_call(core_kernel, out_shape=(out,) * 4, in_specs=[vmem] * 11, o...  11.5 us
    ppermute x1, starting transfers between devices, local(): lax.ppermute(stepped[:1], 'chain', [(i, (i - 1) % count) for i in range(c...  7.66 us
    ppermute x6, waiting for transfers between devices, from_partner(): return lax.ppermute(block, 'chain', [(i, i ^ bits) for i in range(count)])  4.52 us
    ppermute x2, starting transfers between devices, from_row(): lax.ppermute(block, 'mp', [(i, (i + by) % count) for i in range(count)])  4.14 us
    ppermute x6, starting transfers between devices, from_partner(): return lax.ppermute(block, 'chain', [(i, i ^ bits) for i in range(count)])  4.1 us
    dot_general x1, matrix products, local(): shift = jnp.dot(hidden, time_second, preferred_element_type=F32)  1.68 us
    ppermute x1, waiting for transfers between devices, local(): lax.ppermute(stepped[:1], 'chain', [(i, (i - 1) % count) for i in range(c...  1.38 us
    unnamed x1, other arithmetic  0.94 us
  transfers between devices with their start and end apart: 9, of which 5 were waited for; matrix products, arithmetic and copies ran while one was open for 9% of the time, Pallas kernels for 2%

profile of v2, /device:TPU:6, one launch (start us, length us, event | category | flops | bytes accessed | tf_op | source)
XLA Modules:
  0.0 40.7 jit_solution(16577496799937985444)
XLA Ops:
  0.6 0.0 copy-start
  0.6 0.0 copy-start.1
  0.7 0.0 copy-start.7
  0.7 0.0 copy-start.6
  0.7 0.9 %fusion.22 = bf16[4,5,4,64]{3,2,1,0:T(4,128)(2,1)S(1)} fusion(f32[1,4,4,5,64]{4,2,3,1,0:T(4,128)} %param.14), kind=kLoop, calls=%fused_computation.36 | loop fusion | flops 5120 | bytes 30720
  1.6 0.8 %collective-permute-start.1 = (bf16[4,5,4,64]{3,2,1,0:T(4,128)(2,1)S(1)}, bf16[4,5,4,64]{3,2,1,0:T(4,128)(2,1)S(1)}, u32[]{:S(2)}, u32[]{:S(2)}) collective-permute-start(bf16[4,5,4,64]{3,2,1,0:T(4,128)(2,1)S(1)} %fusion.22), channel_id=1, source_target_pairs={{0,7},{1,0},{2,1},{3,2},{4,3},{5,4},{6,5},{7,6},{8,15},{9,8},{10,9... | collective-permute-start | bytes 30728 | tf_op jit(solution)/shard_map/ppermute | solution.py:27
  2.4 3.3 %collective-permute-start = (bf16[4,5,4,64]{3,2,1,0:T(4,128)(2,1)S(1)}, bf16[4,5,4,64]{3,2,1,0:T(4,128)(2,1)S(1)}, u32[]{:S(2)}, u32[]{:S(2)}) collective-permute-start(bf16[4,5,4,64]{3,2,1,0:T(4,128)(2,1)S(1)} %fusion.22), channel_id=1, source_target_pairs={{0,1},{1,2},{2,3},{3,4},{4,5},{5,6},{6,7},{7,0},{8,9},{9,10},{10,1... | collective-permute-start | bytes 30728 | tf_op jit(solution)/shard_map/ppermute | solution.py:27
  5.8 0.8 %bitcast_convert_fusion = bf16[4,5,4,64]{3,2,1,0:T(4,128)(2,1)S(1)} fusion(f32[1,4,4,5,64]{4,2,3,1,0:T(4,128)} %param.14), kind=kLoop, calls=%fused_computation.34 | loop fusion | flops 5120 | bytes 30720 | tf_op jit(solution)/shard_map/convert.7
  6.6 0.7 %convert_element_type.41 = f32[4]{0:T(128)S(1)} convert(s32[4]{0:T(128)} %param.17) | non-fusion elementwise | flops 4 | bytes 32 | tf_op jit(solution)/shard_map/convert_element_type | solution.py:33
  7.2 0.1 fusion.7
  7.3 0.0 copy-done
  7.3 1.7 %reduce-precision_convert_fusion = (bf16[4,320]{1,0:T(4,128)(2,1)S(1)}, bf16[4,320]{1,0:T(4,128)(2,1)S(1)}) fusion(bf16[1280,320]{0,1:T(8,128)(2,1)S(1)} %copy-done, bf16[320,1280]{1,0:T(8,128)(2,1)} %param.20, bf16[4,160]{1,0:T(4,128)(2,1)S(1)} %get-tuple-element.26, bf16[4,160]{1,0:T(4,128)(2,1)S(1)} %get-tuple-element.25), kind=kOutput, calls=%fused_computation.19 | convolution fusion | flops 6589440 | bytes 1646080 | tf_op jit(solution)/shard_map/dot_general | solution.py:303
  9.0 0.1 stack.10
  9.1 0.1 stack.9
  9.3 0.1 convert_element_type.44
  9.3 0.1 pad.18.clone
  9.4 0.0 collective-permute-done.1
  9.4 0.0 collective-permute-done
  9.5 0.1 maximum_maximum_fusion
  9.6 0.1 convert_element_type.40
  9.7 0.1 collective-permute-start.2
  9.8 2.0 %collective-permute-start.3 = (bf16[128,128]{1,0:T(8,128)(2,1)S(1)}, bf16[128,128]{1,0:T(8,128)(2,1)S(1)}, u32[]{:S(2)}, u32[]{:S(2)}) collective-permute-start(bf16[128,128]{1,0:T(8,128)(2,1)S(1)} %fusion.1.s0), channel_id=1, source_target_pairs={{0,16},{8,24},{16,0},{24,8},{32,48},{40,56},{48,32},{56,40},{64,80... | collective-permute-start | bytes 98312 | tf_op jit(solution)/shard_map/ppermute | solution.py:22
  11.8 0.1 collective-permute-start.4
  11.9 0.0 copy-done.1
  11.9 0.0 copy-done.7
  11.9 0.0 copy-done.6
  11.9 0.0 copy-start.2
  11.9 0.0 copy-start.3
  11.9 0.0 copy-start.4
  11.9 0.0 copy-start.5
  11.9 0.9 %shard_map.149 = (bf16[6,320,128]{2,1,0:T(8,128)(2,1)S(1)}, bf16[320,2880]{1,0:T(8,128)(2,1)S(1)}, bf16[48,320]{1,0:T(8,128)(2,1)S(1)}) custom-call(bf16[9,4,320]{2,1,0:T(4,128)(2,1)S(1)} %copy-done.6, bf16[2880,320]{1,0:T(8,128)(2,1)S(1)} %bitcast.40, bf16[9,4,320]{2,1,0:T(4,128)(2,1)S(1)} %bitcast.41), custom_call_target="tpu_custom_call" | custom-call | flops 2000000000 | bytes 6000000 | tf_op jit(solution)/shard_map/pallas_call | solution.py:76
  12.8 0.0 collective-permute-done.2.s1
  12.8 1.0 %collective-permute-done.3.s2 = bf16[128,128]{1,0:T(8,128)(2,1)S(1)} collective-permute-done((bf16[128,128]{1,0:T(8,128)(2,1)S(1)}, bf16[128,128]{1,0:T(8,128)(2,1)S(1)}, u32[]{:S(2)}, u32[]{:S(2)}) %collective-permute-start.3) | collective-permute-done | bytes 32800 | tf_op jit(solution)/shard_map/ppermute | solution.py:22
  13.8 1.4 %collective-permute-done.4.s3 = bf16[128,128]{1,0:T(8,128)(2,1)S(1)} collective-permute-done((bf16[128,128]{1,0:T(8,128)(2,1)S(1)}, bf16[128,128]{1,0:T(8,128)(2,1)S(1)}, u32[]{:S(2)}, u32[]{:S(2)}) %collective-permute-start.4) | collective-permute-done | bytes 32800 | tf_op jit(solution)/shard_map/ppermute | solution.py:22
  15.2 0.0 copy-done.2
  15.2 0.0 copy-done.3
  15.2 0.0 copy-done.4
  15.2 0.0 copy-done.5
  15.2 0.0 copy-start.12
  15.2 0.0 copy-start.8
  15.2 0.0 copy-start.10
  15.2 0.0 copy-start.11
  15.3 11.5 %shard_map.150 = (bf16[48,128]{1,0:T(8,128)(2,1)S(1)}, bf16[48,128]{1,0:T(8,128)(2,1)S(1)}, bf16[48,128]{1,0:T(8,128)(2,1)S(1)}, bf16[48,128]{1,0:T(8,128)(2,1)S(1)}) custom-call(bf16[128,128]{1,0:T(8,128)(2,1)S(1)} %fusion.1.s0, bf16[128,128]{1,0:T(8,128)(2,1)S(1)} %collective-permute-done.2.s1, bf16[128,128]{1,0:T(8,128)(2,1)S(1)} %collective-permute-done.3.s2, ...), custom_call_target="tpu_custom_call" | custom-call | flops 4000000000 | bytes 3000000 | tf_op jit(solution)/shard_map/pallas_call | solution.py:256
  26.7 0.2 collective-permute-start.5
  26.9 0.7 %collective-permute-start.6 = (bf16[48,128]{1,0:T(8,128)(2,1)S(1)}, bf16[48,128]{1,0:T(8,128)(2,1)S(1)}, u32[]{:S(2)}, u32[]{:S(2)}) collective-permute-start(bf16[48,128]{1,0:T(8,128)(2,1)S(1)} %get-tuple-element.14), channel_id=1, source_target_pairs={{0,16},{8,24},{16,0},{24,8},{32,48},{40,56},{48,32},{56,40},{64,80... | collective-permute-start | bytes 36872 | tf_op jit(solution)/shard_map/ppermute | solution.py:22
  27.7 1.0 %collective-permute-start.7 = (bf16[48,128]{1,0:T(8,128)(2,1)S(1)}, bf16[48,128]{1,0:T(8,128)(2,1)S(1)}, u32[]{:S(2)}, u32[]{:S(2)}) collective-permute-start(bf16[48,128]{1,0:T(8,128)(2,1)S(1)} %get-tuple-element.15), channel_id=1, source_target_pairs={{0,24},{8,16},{16,8},{24,0},{32,56},{40,48},{48,40},{56,32},{64,88... | collective-permute-start | bytes 36872 | tf_op jit(solution)/shard_map/ppermute | solution.py:22
  28.7 0.0 copy-done.12
  28.7 0.0 collective-permute-done.5
  28.7 2.0 %collective-permute-done.6 = bf16[48,128]{1,0:T(8,128)(2,1)S(1)} collective-permute-done((bf16[48,128]{1,0:T(8,128)(2,1)S(1)}, bf16[48,128]{1,0:T(8,128)(2,1)S(1)}, u32[]{:S(2)}, u32[]{:S(2)}) %collective-permute-start.6) | collective-permute-done | bytes 12320 | tf_op jit(solution)/shard_map/ppermute | solution.py:22
  30.7 0.1 collective-permute-done.7
  30.8 0.1 fusion.23
  30.9 0.0 copy-done.8
  30.9 0.0 copy-done.10
  30.9 0.1 bitcast_add_fusion
  31.0 0.0 copy-start.9
  31.0 7.7 %collective-permute-start.8 = (f32[1,5,4,64]{3,2,1,0:T(4,128)S(1)}, f32[1,5,4,64]{3,2,1,0:T(4,128)S(1)}, u32[]{:S(2)}, u32[]{:S(2)}) collective-permute-start(f32[1,5,4,64]{3,2,1,0:T(4,128)S(1)} %slice.46), channel_id=1, source_target_pairs={{0,248},{8,0},{16,8},{24,16},{32,24},{40,32},{48,40},{56,48},{64,5... | collective-permute-start | bytes 15368 | tf_op jit(solution)/shard_map/ppermute | solution.py:328
  38.7 1.4 %collective-permute-done.8 = f32[1,5,4,64]{3,2,1,0:T(4,128)S(1)} collective-permute-done((f32[1,5,4,64]{3,2,1,0:T(4,128)S(1)}, f32[1,5,4,64]{3,2,1,0:T(4,128)S(1)}, u32[]{:S(2)}, u32[]{:S(2)}) %collective-permute-start.8) | collective-permute-done | bytes 5152 | tf_op jit(solution)/shard_map/ppermute | solution.py:328
  40.1 0.0 copy-done.11
  40.1 0.6 %maximum_bitcast_fusion = f32[1,4,4,5,64]{4,2,3,1,0:T(4,128)} fusion(f32[1,5,4,64]{3,2,1,0:T(4,128)S(1)} %bitcast_select_fusion, f32[3,5,4,64]{3,2,1,0:T(4,128)S(1)} %slice.45), kind=kLoop, calls=%fused_computation.5 | loop fusion | flops 5120 | bytes 40960 | tf_op jit(solution)/shard_map/broadcast_in_dim | solution.py:332
  40.7 0.0 copy-done.9
  (13 shorter events, 0.1 us)
Async XLA Ops:
  0.6 6.7 %copy-start = (bf16[1280,320]{0,1:T(8,128)(2,1)S(1)}, bf16[1280,320]{0,1:T(8,128)(2,1)}, u32[]{:S(2)}) copy-start(bf16[1280,320]{0,1:T(8,128)(2,1)} %param.21) | copy-start | bytes 2457604
  0.6 11.2 %copy-start.1 = (bf16[9,320,320]{2,1,0:T(8,128)(2,1)S(1)}, bf16[9,320,320]{2,1,0:T(8,128)(2,1)}, u32[]{:S(2)}) copy-start(bf16[9,320,320]{2,1,0:T(8,128)(2,1)} %param.22) | copy-start | bytes 5529604
  0.7 11.2 %copy-start.7 = (bf16[9,320,4]{1,2,0:T(4,128)(2,1)S(1)}, bf16[9,320,4]{1,2,0:T(4,128)(2,1)}, u32[]{:S(2)}) copy-start(bf16[9,320,4]{1,2,0:T(4,128)(2,1)} %param.27) | copy-start | bytes 69124
  0.7 11.2 %copy-start.6 = (bf16[9,4,320]{2,1,0:T(4,128)(2,1)S(1)}, bf16[9,4,320]{2,1,0:T(4,128)(2,1)}, u32[]{:S(2)}) copy-start(bf16[9,4,320]{2,1,0:T(4,128)(2,1)} %inlet.1) | copy-start | bytes 69124
  1.6 7.8 %collective-permute-start.1 = (bf16[4,5,4,64]{3,2,1,0:T(4,128)(2,1)S(1)}, bf16[4,5,4,64]{3,2,1,0:T(4,128)(2,1)S(1)}, u32[]{:S(2)}, u32[]{:S(2)}) collective-permute-start(bf16[4,5,4,64]{3,2,1,0:T(4,128)(2,1)S(1)} %fusion.22), channel_id=1, source_target_pairs={{0,7},{1,0},{2,1},{3,2},{4,3},{5,4},{6,5},{7,6},{8,15},{9,8},{10,9... | collective-permute-start | bytes 30728 | tf_op jit(solution)/shard_map/ppermute | solution.py:27
  2.4 7.0 %collective-permute-start = (bf16[4,5,4,64]{3,2,1,0:T(4,128)(2,1)S(1)}, bf16[4,5,4,64]{3,2,1,0:T(4,128)(2,1)S(1)}, u32[]{:S(2)}, u32[]{:S(2)}) collective-permute-start(bf16[4,5,4,64]{3,2,1,0:T(4,128)(2,1)S(1)} %fusion.22), channel_id=1, source_target_pairs={{0,1},{1,2},{2,3},{3,4},{4,5},{5,6},{6,7},{7,0},{8,9},{9,10},{10,1... | collective-permute-start | bytes 30728 | tf_op jit(solution)/shard_map/ppermute | solution.py:27
  9.7 3.1 %collective-permute-start.2 = (bf16[128,128]{1,0:T(8,128)(2,1)S(1)}, bf16[128,128]{1,0:T(8,128)(2,1)S(1)}, u32[]{:S(2)}, u32[]{:S(2)}) collective-permute-start(bf16[128,128]{1,0:T(8,128)(2,1)S(1)} %fusion.1.s0), channel_id=1, source_target_pairs={{0,8},{8,0},{16,24},{24,16},{32,40},{40,32},{48,56},{56,48},{64,72... | collective-permute-start | bytes 98312 | tf_op jit(solution)/shard_map/ppermute | solution.py:22
  9.8 4.0 %collective-permute-start.3 = (bf16[128,128]{1,0:T(8,128)(2,1)S(1)}, bf16[128,128]{1,0:T(8,128)(2,1)S(1)}, u32[]{:S(2)}, u32[]{:S(2)}) collective-permute-start(bf16[128,128]{1,0:T(8,128)(2,1)S(1)} %fusion.1.s0), channel_id=1, source_target_pairs={{0,16},{8,24},{16,0},{24,8},{32,48},{40,56},{48,32},{56,40},{64,80... | collective-permute-start | bytes 98312 | tf_op jit(solution)/shard_map/ppermute | solution.py:22
  11.8 3.4 %collective-permute-start.4 = (bf16[128,128]{1,0:T(8,128)(2,1)S(1)}, bf16[128,128]{1,0:T(8,128)(2,1)S(1)}, u32[]{:S(2)}, u32[]{:S(2)}) collective-permute-start(bf16[128,128]{1,0:T(8,128)(2,1)S(1)} %fusion.1.s0), channel_id=1, source_target_pairs={{0,24},{8,16},{16,8},{24,0},{32,56},{40,48},{48,40},{56,32},{64,88... | collective-permute-start | bytes 98312 | tf_op jit(solution)/shard_map/ppermute | solution.py:22
  11.9 3.3 %copy-start.2 = (bf16[320,320]{1,0:T(8,128)(2,1)S(1)}, bf16[320,320]{1,0:T(8,128)(2,1)}, u32[]{:S(2)}) copy-start(bf16[320,320]{1,0:T(8,128)(2,1)} %wq.1) | copy-start | bytes 614404
  11.9 3.3 %copy-start.3 = (bf16[320,320]{1,0:T(8,128)(2,1)S(1)}, bf16[320,320]{1,0:T(8,128)(2,1)}, u32[]{:S(2)}) copy-start(bf16[320,320]{1,0:T(8,128)(2,1)} %wk.1) | copy-start | bytes 614404
  11.9 3.3 %copy-start.4 = (bf16[320,320]{1,0:T(8,128)(2,1)S(1)}, bf16[320,320]{1,0:T(8,128)(2,1)}, u32[]{:S(2)}) copy-start(bf16[320,320]{1,0:T(8,128)(2,1)} %wv.1) | copy-start | bytes 614404
  11.9 3.3 %copy-start.5 = (bf16[320,320]{1,0:T(8,128)(2,1)S(1)}, bf16[320,320]{1,0:T(8,128)(2,1)}, u32[]{:S(2)}) copy-start(bf16[320,320]{1,0:T(8,128)(2,1)} %wo_in.1) | copy-start | bytes 614404
  15.2 13.5 %copy-start.12 = (f32[3,4]{1,0:T(4,128)S(1)}, f32[3,4]{1,0:T(4,128)}, u32[]{:S(2)}) copy-start(f32[3,4]{1,0:T(4,128)} %param.18) | copy-start | bytes 148
  15.2 15.7 %copy-start.8 = (f32[1,4,4,5,64]{4,2,3,1,0:T(4,128)S(1)}, f32[1,4,4,5,64]{4,2,3,1,0:T(4,128)}, u32[]{:S(2)}) copy-start(f32[1,4,4,5,64]{4,2,3,1,0:T(4,128)} %param.14) | copy-start | bytes 61444
  15.2 15.7 %copy-start.10 = (f32[1,4,4,5,64]{4,2,3,1,0:T(4,128)S(1)}, f32[1,4,4,5,64]{4,2,3,1,0:T(4,128)}, u32[]{:S(2)}) copy-start(f32[1,4,4,5,64]{4,2,3,1,0:T(4,128)} %param.15) | copy-start | bytes 61444
  15.2 24.9 %copy-start.11 = (f32[1,4,5,64]{3,1,2,0:T(4,128)S(1)}, f32[1,4,5,64]{3,1,2,0:T(4,128)}, u32[]{:S(2)}) copy-start(f32[1,4,5,64]{3,1,2,0:T(4,128)} %param.16) | copy-start | bytes 15364
  26.7 2.0 %collective-permute-start.5 = (bf16[48,128]{1,0:T(8,128)(2,1)S(1)}, bf16[48,128]{1,0:T(8,128)(2,1)S(1)}, u32[]{:S(2)}, u32[]{:S(2)}) collective-permute-start(bf16[48,128]{1,0:T(8,128)(2,1)S(1)} %get-tuple-element.13), channel_id=1, source_target_pairs={{0,8},{8,0},{16,24},{24,16},{32,40},{40,32},{48,56},{56,48},{64,72... | collective-permute-start | bytes 36872 | tf_op jit(solution)/shard_map/ppermute | solution.py:22
  26.9 3.7 %collective-permute-start.6 = (bf16[48,128]{1,0:T(8,128)(2,1)S(1)}, bf16[48,128]{1,0:T(8,128)(2,1)S(1)}, u32[]{:S(2)}, u32[]{:S(2)}) collective-permute-start(bf16[48,128]{1,0:T(8,128)(2,1)S(1)} %get-tuple-element.14), channel_id=1, source_target_pairs={{0,16},{8,24},{16,0},{24,8},{32,48},{40,56},{48,32},{56,40},{64,80... | collective-permute-start | bytes 36872 | tf_op jit(solution)/shard_map/ppermute | solution.py:22
  27.7 3.1 %collective-permute-start.7 = (bf16[48,128]{1,0:T(8,128)(2,1)S(1)}, bf16[48,128]{1,0:T(8,128)(2,1)S(1)}, u32[]{:S(2)}, u32[]{:S(2)}) collective-permute-start(bf16[48,128]{1,0:T(8,128)(2,1)S(1)} %get-tuple-element.15), channel_id=1, source_target_pairs={{0,24},{8,16},{16,8},{24,0},{32,56},{40,48},{48,40},{56,32},{64,88... | collective-permute-start | bytes 36872 | tf_op jit(solution)/shard_map/ppermute | solution.py:22
  31.0 9.7 %copy-start.9 = (f32[4,5,4,64]{3,2,1,0:T(4,128)}, f32[4,5,4,64]{3,2,1,0:T(4,128)S(1)}, u32[]{:S(2)}) copy-start(f32[4,5,4,64]{3,2,1,0:T(4,128)S(1)} %bitcast_add_fusion) | copy-start | bytes 61444
  31.0 9.0 %collective-permute-start.8 = (f32[1,5,4,64]{3,2,1,0:T(4,128)S(1)}, f32[1,5,4,64]{3,2,1,0:T(4,128)S(1)}, u32[]{:S(2)}, u32[]{:S(2)}) collective-permute-start(f32[1,5,4,64]{3,2,1,0:T(4,128)S(1)} %slice.46), channel_id=1, source_target_pairs={{0,248},{8,0},{16,8},{24,16},{32,24},{40,32},{48,40},{56,48},{64,5... | collective-permute-start | bytes 15368 | tf_op jit(solution)/shard_map/ppermute | solution.py:328

commit v3 on v2

--- a/solution.py
+++ b/solution.py
@@ -46,11 +46,35 @@
     return lax.broadcasted_iota(jnp.int32, shape, dim)
 
 
+def select(where, a, b):
+    return jnp.where(jnp.broadcast_to(where, a.shape), a, b)
+
+
 def mm(a, b):
     return jnp.dot(a, b, preferred_element_type=F32)
 
 
-def prep_kernel(inlet, wres, outlet, win_t, wres_t, wout_t, rows):
+def prep_kernel(inlet, wres, outlet, win_t, wres_t, wout_t, gather, pick, scatter, rows):
+    tile = lax.axis_index("chain") % GROUP
+    lane = iota((128, 384), 1)
+    cell, slot, block = lane % 8, lane % 128 // 8, lane // 128
+    at = jnp.where(
+        block < 2,
+        16 * tile + 8 * block + cell,
+        jnp.where(cell == 0, 16 * tile - 1, jnp.where(cell == 7, 16 * tile + 16, -1000)),
+    )
+    src = iota((128, 384), 0)
+    same_half = src // 64 == slot % 2
+    for dx in range(3):
+        gather[dx] = (same_half & (src % 64 == at + (dx - 1))).astype(F32).astype(BF16)
+    er, el = iota((128, 640), 0), iota((128, 640), 1)
+    spot = (er % 32 // 4 == el // 128) & (er // 32 * 4 + er % 4 == el % 128 // 8)
+    pick[...] = spot.astype(F32).astype(BF16)
+    src, dst = iota((256, 128), 0), iota((256, 128), 1)
+    same_half = src % 128 // 8 % 2 == dst // 64
+    spot = 16 * tile + src // 128 * 8 + src % 8 - dst % 64
+    for b in range(3):
+        scatter[b] = (same_half & (spot == b - 1)).astype(F32).astype(BF16)
     rows[...] = jnp.zeros_like(rows)
     for dy in range(3):
         for dx in range(3):
@@ -72,12 +96,12 @@
 
 def prep(inlet, wres, outlet):
     vmem = pl.BlockSpec(memory_space=pltpu.VMEM)
-    shapes = ((6, C, 128), (C, 9 * C), (48, C))
+    shapes = ((6, C, 128), (C, 9 * C), (48, C), (3, 128, 384), (128, 640), (3, 256, 128))
     return pl.pallas_call(
         prep_kernel,
         out_shape=tuple(jax.ShapeDtypeStruct(s, BF16) for s in shapes),
         in_specs=[vmem] * 3,
-        out_specs=(vmem,) * 3,
+        out_specs=(vmem,) * 6,
         scratch_shapes=[pltpu.VMEM((128, C), F32)],
         compiler_params=pltpu.CompilerParams(vmem_limit_bytes=32 * 1024 * 1024),
         cost_estimate=pl.CostEstimate(
@@ -87,38 +111,26 @@
 
 
 def core_kernel(
-    s0, s1, s2, s3, win, wres, wq, wk, wv, wo_in, wout,
+    s0, s1, s2, s3, win, wres, wq, wk, wv, wo_in, wout, gather, pick, scatter,
     o0, o1, o2, o3,
-    opn, act, res, nrm, qkv, scr, att, accs, wqkv, wo,
+    opn, act, res, nrm, qkv, scr, att, accs, wqkv, wo, pairs,
 ):
     tile = lax.axis_index("chain") % GROUP
     row_block = lax.axis_index("mp")
     last_row = lax.axis_size("mp") - 1
     slabs = [s0[...], s1[...], s2[...], s3[...]]
     shift_rows = jnp.concatenate([s[96:128] for s in slabs], axis=0)
-    er, el = iota((128, 640), 0), iota((128, 640), 1)
-    pick = (er % 32 // 4 == el // 128) & (er // 32 * 4 + er % 4 == el % 128 // 8)
-    spread = mm(shift_rows.astype(F32).T.astype(BF16), pick.astype(F32).astype(BF16))
+    spread = mm(shift_rows.astype(F32).T.astype(BF16), pick[...])
     spread = spread[:64] + spread[64:]
     shift = jnp.concatenate([spread[:, 128 * i : 128 * i + 128] for i in range(5)], axis=0) * 0.5
     latent = jnp.concatenate([s[:96] for s in slabs], axis=0)
-    lane = iota((128, 384), 1)
-    cell, slot, block = lane % 8, lane % 128 // 8, lane // 128
-    at = jnp.where(
-        block < 2,
-        16 * tile + 8 * block + cell,
-        jnp.where(cell == 0, 16 * tile - 1, jnp.where(cell == 7, 16 * tile + 16, -1000)),
-    )
-    src = iota((128, 384), 0)
-    same_half = src // 64 == slot % 2
     pair_of = iota((1, 1, 384), 2) % 128 // 16
     pair_no = iota((8, 1, 384), 0)
     row_of = iota((48, 384), 0) // 4
     inside = ((row_block > 0) | (row_of >= 3)) & ((row_block < last_row) | (row_of < 3 + ROWS))
     columns = []
     for dx in range(3):
-        chosen = same_half & (src % 64 == at + (dx - 1))
-        moved = mm(latent, chosen.astype(F32).astype(BF16))
+        moved = mm(latent, gather[dx])
         moved = jnp.where(pair_of == pair_no, moved.reshape(8, 48, 384), 0.0)
         columns.append(jnp.where(inside, jnp.sum(moved, axis=0), 0.0))
     empty = jnp.zeros((32, 384), F32)
@@ -151,20 +163,16 @@
             if r > ROWS + 1:
                 part = part * jnp.where(row_block < last_row, 1.0, 0.0)
             parts.append(part)
-        a0, a1, edge = parts
+        a0, a1, edge = [part.astype(BF16) for part in parts]
         base = 960 * r
-        act[base : base + 320, :128] = jnp.where(first, edge, pltpu.roll(a0, 1, 1)).astype(BF16)
-        act[base : base + 320, 128:] = jnp.where(
-            first, pltpu.roll(a0, 121, 1), pltpu.roll(a1, 1, 1)
-        ).astype(BF16)
-        act[base + 320 : base + 640, :128] = a0.astype(BF16)
-        act[base + 320 : base + 640, 128:] = a1.astype(BF16)
-        act[base + 640 : base + 960, :128] = jnp.where(
+        act[base : base + 320, :128] = select(first, edge, pltpu.roll(a0, 1, 1))
+        act[base : base + 320, 128:] = select(first, pltpu.roll(a0, 121, 1), pltpu.roll(a1, 1, 1))
+        act[base + 320 : base + 640, :128] = a0
+        act[base + 320 : base + 640, 128:] = a1
+        act[base + 640 : base + 960, :128] = select(
             last, pltpu.roll(a1, 7, 1), pltpu.roll(a0, 127, 1)
-        ).astype(BF16)
-        act[base + 640 : base + 960, 128:] = jnp.where(
-            last, edge, pltpu.roll(a1, 127, 1)
-        ).astype(BF16)
+        )
+        act[base + 640 : base + 960, 128:] = select(last, edge, pltpu.roll(a1, 127, 1))
 
     def convolve(r):
         residual = opn[r + 1, :, :256] + mm(wres[...], act[960 * r : 960 * r + 2880, :])
@@ -172,18 +180,28 @@
         nrm[r] = (residual * inv_rms(residual)).astype(BF16)
 
     def project(r):
-        qkv[r] = mm(wqkv[...], nrm[r]).astype(BF16)
+        full = mm(wqkv[...], nrm[r]).astype(BF16)
+        qkv[r] = full[C:]
+        for b in range(2):
+            for h in range(HEADS):
+                at = h % 2
+                pairs[r % 2, b, h // 2, 64 * at : 64 * at + 64, 128 * at : 128 * at + 128] = full[
+                    64 * h : 64 * h + 64, 128 * b : 128 * b + 128
+                ]
 
     def score(r):
         for b in range(2):
-            piece = slice(128 * b, 128 * b + 128)
-            for h in range(HEADS):
-                scr[r % 2, HEADS * b + h] = lax.dot_general(
-                    qkv[r, 320 + 64 * h : 384 + 64 * h, piece],
-                    qkv[r, 64 * h : 64 * h + 64, piece],
+            for p in range(3):
+                heads = min(2, HEADS - 2 * p)
+                wide = lax.dot_general(
+                    qkv[r, 128 * p : 128 * p + 64 * heads, 128 * b : 128 * b + 128],
+                    pairs[r % 2, b, p, : 64 * heads, : 128 * heads],
                     (((0,), (0,)), ((), ())),
                     preferred_element_type=F32,
-                ).reshape(16, 8, 128)
+                )
+                for i in range(heads):
+                    part = wide[:, 128 * i : 128 * i + 128]
+                    scr[r % 2, HEADS * b + 2 * p + i] = part.reshape(16, 8, 128)
 
     def attend(r):
         probs = []
@@ -196,7 +214,7 @@
         for b in range(2):
             piece = slice(128 * b, 128 * b + 128)
             for h in range(HEADS):
-                value = qkv[r, 640 + 64 * h : 704 + 64 * h, piece]
+                value = qkv[r, C + 64 * h : C + 64 * h + 64, piece]
                 att[r, 64 * h : 64 * h + 64, piece] = mm(value, probs[HEADS * b + h]).astype(BF16)
 
     def mix(r):
@@ -215,11 +233,12 @@
                 accs[r - a] += taps[16 * a : 16 * a + 16]
 
     accs[...] = jnp.zeros_like(accs)
+    pairs[...] = jnp.zeros_like(pairs)
     for i, w in enumerate((wq, wk, wv)):
         wqkv[C * i : C * i + C, :] = w[...].T
     wo[...] = wo_in[...].T
     count = ROWS + 2
-    for r in range(count + 2):
+    for r in range(4):
         open_row(r)
     for r in range(3):
         activate(r)
@@ -228,53 +247,51 @@
             convolve(step)
             if step < count - 1:
                 activate(step + 3)
+            if step < count - 2:
+                open_row(step + 4)
         for late, stage in enumerate((project, score, attend, mix, outlet), 1):
             if 0 <= step - late < count:
                 stage(step - late)
-    src = iota((256, 128), 0)
-    dst = iota((256, 128), 1)
-    same_half = src % 128 // 8 % 2 == dst // 64
-    spot = 16 * tile + src // 128 * 8 + src % 8 - dst % 64
     pair_of = iota((1, 1, 256), 2) % 128 // 16
     pair_no = iota((8, 1, 256), 0)
     total = None
     for b in range(3):
-        chosen = (same_half & (spot == b - 1)).astype(F32).astype(BF16)
         part = accs[:, 4 * b : 4 * b + 4, :].reshape(24, 256)
         high = part.astype(BF16).astype(F32)
         for piece in (high, part - high):
             wide = jnp.where(pair_of == pair_no, piece[None], 0.0)
-            term = mm(wide.reshape(192, 256).astype(BF16), chosen)
+            term = mm(wide.reshape(192, 256).astype(BF16), scatter[b])
             total = term if total is None else total + term
     for k, out in enumerate((o0, o1, o2, o3)):
         out[...] = total[48 * k : 48 * k + 48].astype(BF16)
 
 
-def core(slabs, win, wres, wq, wk, wv, wo, wout):
+def core(slabs, win, wres, wq, wk, wv, wo, wout, gather, pick, scatter):
     out = jax.ShapeDtypeStruct((48, 128), BF16)
     vmem = pl.BlockSpec(memory_space=pltpu.VMEM)
     return pl.pallas_call(
         core_kernel,
         out_shape=(out,) * 4,
-        in_specs=[vmem] * 11,
+        in_specs=[vmem] * 14,
         out_specs=(vmem,) * 4,
         scratch_shapes=[
             pltpu.VMEM((ROWS + 4, C, 384), F32),
             pltpu.VMEM(((ROWS + 4) * 960, 256), BF16),
             pltpu.VMEM((ROWS + 2, C, 256), F32),
             pltpu.VMEM((ROWS + 2, C, 256), BF16),
-            pltpu.VMEM((ROWS + 2, 3 * C, 256), BF16),
+            pltpu.VMEM((ROWS + 2, 2 * C, 256), BF16),
             pltpu.VMEM((2, 10, 16, 8, 128), F32),
             pltpu.VMEM((ROWS + 2, C, 256), BF16),
             pltpu.VMEM((ROWS + 1, 16, 256), F32),
             pltpu.VMEM((3 * C, C), BF16),
             pltpu.VMEM((C, C), BF16),
+            pltpu.VMEM((2, 2, 3, 128, 256), BF16),
         ],
         compiler_params=pltpu.CompilerParams(vmem_limit_bytes=36 * 1024 * 1024),
         cost_estimate=pl.CostEstimate(
             flops=4_000_000_000, bytes_accessed=3_000_000, transcendentals=3_000_000
         ),
-    )(*slabs, win, wres, wq, wk, wv, wo, wout)
+    )(*slabs, win, wres, wq, wk, wv, wo, wout, gather, pick, scatter)
 
 
 def local(
@@ -296,8 +313,9 @@
     latent = jnp.transpose(latents[0], (0, 2, 1, 3))
     noise = jnp.transpose(step_noise[0], (0, 2, 1, 3))
     fresh = jnp.transpose(fresh_noise, (0, 2, 1, 3))
-    below = from_row(latent, 1)[:, ROWS - 3 :]
-    above = from_row(latent, -1)[:, :3]
+    narrow = lax.optimization_barrier(latent.astype(BF16))
+    below = from_row(narrow, 1)[:, ROWS - 3 :]
+    above = from_row(narrow, -1)[:, :3]
     embedded = embed_steps(timesteps).astype(BF16)
     hidden = jax.nn.silu(jnp.dot(embedded, time_first, preferred_element_type=F32)).astype(BF16)
     shift = jnp.dot(hidden, time_second, preferred_element_type=F32)
@@ -305,18 +323,20 @@
     split = jnp.stack([high, shift - high]).reshape(2, 4, 5, 64)
     split = jnp.transpose(split, (2, 1, 0, 3)).reshape(20, 128).astype(BF16)
     split = jnp.pad(split, ((0, 12), (0, 0)))
-    rows = jnp.concatenate([below, latent, above, jnp.zeros_like(latent[:, :1])], axis=1)
-    rows = jnp.transpose(rows.reshape(2, 2, 48, 64), (0, 2, 1, 3)).reshape(96, 128).astype(BF16)
+    rows = jnp.concatenate([below, narrow, above, jnp.zeros_like(narrow[:, :1])], axis=1)
+    rows = jnp.transpose(rows.reshape(2, 2, 48, 64), (0, 2, 1, 3)).reshape(96, 128)
     slab = jnp.concatenate([rows, split], axis=0)
-    slabs = [slab] + [from_partner(slab, k) for k in (1, 2, 3)]
-    win, wres, wout = prep(
+    far, across, near = [from_partner(slab, k) for k in (3, 2, 1)]
+    slabs = (slab, near, across, far)
+    win, wres, wout, *moves = prep(
         inlet_weight, res_weight.reshape(9 * C, C), jnp.transpose(outlet_weight, (0, 2, 1))
     )
     squares = (query_weight, key_weight, value_weight, output_weight)
-    sent = core(slabs, win, wres, *squares, wout)
+    sent = core(slabs, win, wres, *squares, wout, *moves)
     total = sent[0].astype(F32)
-    for k in (1, 2, 3):
-        total = total + from_partner(sent[k], k).astype(F32)
+    arrived = [from_partner(sent[k], k) for k in (3, 2, 1)]
+    for part in arrived:
+        total = total + part.astype(F32)
     middle = total.reshape(2, 6, 4, 128)[:, :ROWS]
     predicted = jnp.transpose(middle.reshape(2, 5, 4, 2, 64), (0, 3, 1, 2, 4)).reshape(4, 5, 4, 64)
 

time: 41 us -> 39.3 us (0.959)
  starting transfers between devices: 15.9 us -> 12.1 us
  waiting for transfers between devices: 5.91 us -> 7.46 us
  local copies, waits for them, and re-layouts: 0.68 us -> 2.15 us
  other arithmetic: 3.38 us -> 2.59 us
    ppermute x2, waiting for transfers between devices: 0.01 us -> 2.46 us  [from_row(): lax.ppermute(block, 'mp', [(i, (i + by) % count) for i in range(count)])]
    ppermute x2, starting transfers between devices: 4.14 us -> 2.03 us  [from_row(): lax.ppermute(block, 'mp', [(i, (i + by) % count) for i in range(count)])]
    ppermute x1, starting transfers between devices: 7.66 us -> 5.98 us  [local(): lax.ppermute(stepped[:1], 'chain', [(i, (i - 1) % count) for i in range(c...]
    unnamed x26, local copies, waits for them, and re-layouts: 0.08 us -> 1.55 us
    convert_element_type x0 -> x1, other arithmetic: none -> 0.94 us  [local(): narrow = lax.optimization_barrier(latent.astype(BF16))]
    unnamed x1 -> x0, other arithmetic: 0.94 us -> none
    ppermute x6, waiting for transfers between devices: 4.52 us -> 3.61 us  [from_partner(): return lax.ppermute(block, 'chain', [(i, i ^ bits) for i in range(count)])]
    another operation x2 -> x1, other arithmetic: 0.91 us -> 0.12 us
  transfers between devices with their start and end apart: 9 -> 9, of which waited for: 5 -> 5; matrix products, arithmetic and copies ran while one was open for 9% -> 7% of each run, Pallas kernels for 2% -> 3%
where the time goes in v3:
time: 39.3 us; the launch traced here: 39 us
  Pallas kernels  12.2 us (31%)
  starting transfers between devices  12.1 us (31%)
  waiting for transfers between devices  7.46 us (19%)
  other arithmetic  2.59 us (7%)
  local copies, waits for them, and re-layouts  2.15 us (5%)
  matrix products  1.68 us (4%)
  between operations  0.86 us (2%)
    pallas_call x1, Pallas kernels, core(): pl.pallas_call(core_kernel, out_shape=(out,) * 4, in_specs=[vmem] * 14, o...  11.1 us
    ppermute x1, starting transfers between devices, local(): lax.ppermute(stepped[:1], 'chain', [(i, (i - 1) % count) for i in range(c...  5.98 us
    ppermute x6, starting transfers between devices, from_partner(): return lax.ppermute(block, 'chain', [(i, i ^ bits) for i in range(count)])  4.1 us
    ppermute x6, waiting for transfers between devices, from_partner(): return lax.ppermute(block, 'chain', [(i, i ^ bits) for i in range(count)])  3.61 us
    ppermute x2, waiting for transfers between devices, from_row(): lax.ppermute(block, 'mp', [(i, (i + by) % count) for i in range(count)])  2.46 us
    ppermute x2, starting transfers between devices, from_row(): lax.ppermute(block, 'mp', [(i, (i + by) % count) for i in range(count)])  2.03 us
    dot_general x1, matrix products, local(): shift = jnp.dot(hidden, time_second, preferred_element_type=F32)  1.68 us
    unnamed x26, local copies, waits for them, and re-layouts  1.55 us
  transfers between devices with their start and end apart: 9, of which 5 were waited for; matrix products, arithmetic and copies ran while one was open for 7% of the time, Pallas kernels for 3%

profile of v3, /device:TPU:6, one launch (start us, length us, event | category | flops | bytes accessed | tf_op | source)
XLA Modules:
  0.0 39.0 jit_solution(1291864072287580990)
XLA Ops:
  0.6 0.0 copy-start
  0.6 0.0 copy-start.1
  0.7 0.9 %fusion.2 = bf16[4,5,4,64]{3,2,1,0:T(4,128)(2,1)S(1)} fusion(f32[1,4,4,5,64]{4,2,3,1,0:T(4,128)} %param.14), kind=kLoop, calls=%fused_computation.14 | loop fusion | flops 5120 | bytes 30720 | tf_op jit(solution)/shard_map/convert_element_type | solution.py:316
  1.6 1.5 %collective-permute-start = (bf16[4,5,4,64]{3,2,1,0:T(4,128)(2,1)S(1)}, bf16[4,5,4,64]{3,2,1,0:T(4,128)(2,1)S(1)}, u32[]{:S(2)}, u32[]{:S(2)}) collective-permute-start(bf16[4,5,4,64]{3,2,1,0:T(4,128)(2,1)S(1)} %fusion.2), channel_id=1, source_target_pairs={{0,1},{1,2},{2,3},{3,4},{4,5},{5,6},{6,7},{7,0},{8,9},{9,10},{10,1... | collective-permute-start | bytes 30728 | tf_op jit(solution)/shard_map/ppermute | solution.py:27
  3.1 0.5 %collective-permute-start.1 = (bf16[4,5,4,64]{3,2,1,0:T(4,128)(2,1)S(1)}, bf16[4,5,4,64]{3,2,1,0:T(4,128)(2,1)S(1)}, u32[]{:S(2)}, u32[]{:S(2)}) collective-permute-start(bf16[4,5,4,64]{3,2,1,0:T(4,128)(2,1)S(1)} %fusion.2), channel_id=1, source_target_pairs={{0,7},{1,0},{2,1},{3,2},{4,3},{5,4},{6,5},{7,6},{8,15},{9,8},{10,9... | collective-permute-start | bytes 30728 | tf_op jit(solution)/shard_map/ppermute | solution.py:27
  3.6 0.7 %convert_element_type.36 = f32[4]{0:T(128)S(1)} convert(s32[4]{0:T(128)} %param.17) | non-fusion elementwise | flops 4 | bytes 32 | tf_op jit(solution)/shard_map/convert_element_type | solution.py:33
  4.3 0.1 fusion.8
  4.4 0.0 copy-done
  4.4 1.7 %reduce-precision_convert_fusion = (bf16[4,320]{1,0:T(4,128)(2,1)S(1)}, bf16[4,320]{1,0:T(4,128)(2,1)S(1)}) fusion(bf16[1280,320]{0,1:T(8,128)(2,1)S(1)} %copy-done, bf16[320,1280]{1,0:T(8,128)(2,1)} %param.20, bf16[4,160]{1,0:T(4,128)(2,1)S(1)} %get-tuple-element.30, bf16[4,160]{1,0:T(4,128)(2,1)S(1)} %get-tuple-element.29), kind=kOutput, calls=%fused_computation.21 | convolution fusion | flops 6589440 | bytes 1646080 | tf_op jit(solution)/shard_map/dot_general | solution.py:321
  6.1 0.1 stack.10
  6.2 0.1 stack.9
  6.3 0.1 convert_element_type.39
  6.4 0.1 pad.18.clone
  6.5 0.0 collective-permute-done
  6.5 2.5 %collective-permute-done.1 = bf16[4,5,4,64]{3,2,1,0:T(4,128)(2,1)S(1)} collective-permute-done((bf16[4,5,4,64]{3,2,1,0:T(4,128)(2,1)S(1)}, bf16[4,5,4,64]{3,2,1,0:T(4,128)(2,1)S(1)}, u32[]{:S(2)}, u32[]{:S(2)}) %collective-permute-start.1) | collective-permute-done | bytes 10272 | tf_op jit(solution)/shard_map/ppermute | solution.py:27
  9.0 0.1 maximum_maximum_fusion
  9.1 0.1 reshape.39
  9.2 0.1 collective-permute-start.2
  9.3 2.0 %collective-permute-start.3 = (bf16[128,128]{1,0:T(8,128)(2,1)S(1)}, bf16[128,128]{1,0:T(8,128)(2,1)S(1)}, u32[]{:S(2)}, u32[]{:S(2)}) collective-permute-start(bf16[128,128]{1,0:T(8,128)(2,1)S(1)} %fusion.1.s0), channel_id=1, source_target_pairs={{0,16},{8,24},{16,0},{24,8},{32,48},{40,56},{48,32},{56,40},{64,80... | collective-permute-start | bytes 98312 | tf_op jit(solution)/shard_map/ppermute | solution.py:22
  11.3 0.1 collective-permute-start.4
  11.4 0.0 copy-done.1
  11.4 0.0 copy-start.6
  11.4 0.7 %copy-done.6 = bf16[9,4,320]{2,1,0:T(4,128)(2,1)S(1)} copy-done((bf16[9,4,320]{2,1,0:T(4,128)(2,1)S(1)}, bf16[9,4,320]{2,1,0:T(4,128)(2,1)}, u32[]{:S(2)}) %copy-start.6) | copy-done | bytes 23064
  12.1 0.0 copy-start.7
  12.1 0.7 %copy-done.7 = bf16[9,320,4]{1,2,0:T(4,128)(2,1)S(1)} copy-done((bf16[9,320,4]{1,2,0:T(4,128)(2,1)S(1)}, bf16[9,320,4]{1,2,0:T(4,128)(2,1)}, u32[]{:S(2)}) %copy-start.7) | copy-done | bytes 23064
  12.9 0.0 copy-start.2
  12.9 0.0 copy-start.3
  12.9 0.0 copy-start.4
  12.9 0.0 copy-start.5
  12.9 1.1 %shard_map.149 = (bf16[6,320,128]{2,1,0:T(8,128)(2,1)S(1)}, bf16[320,2880]{1,0:T(8,128)(2,1)S(1)}, bf16[48,320]{1,0:T(8,128)(2,1)S(1)}, bf16[3,128,384]{2,1,0:T(...) custom-call(bf16[9,4,320]{2,1,0:T(4,128)(2,1)S(1)} %copy-done.6, ...), custom_call_target="tpu_custom_call" | custom-call | flops 2000000000 | bytes 6000000 | tf_op jit(solution)/shard_map/pallas_call | solution.py:100
  14.0 0.0 collective-permute-done.2.s1
  14.0 0.0 collective-permute-done.3.s2
  14.1 0.6 %collective-permute-done.4.s3 = bf16[128,128]{1,0:T(8,128)(2,1)S(1)} collective-permute-done((bf16[128,128]{1,0:T(8,128)(2,1)S(1)}, bf16[128,128]{1,0:T(8,128)(2,1)S(1)}, u32[]{:S(2)}, u32[]{:S(2)}) %collective-permute-start.4) | collective-permute-done | bytes 32800 | tf_op jit(solution)/shard_map/ppermute | solution.py:22
  14.7 0.0 copy-done.2
  14.7 0.0 copy-done.3
  14.7 0.0 copy-done.4
  14.7 0.0 copy-done.5
  14.7 0.0 copy-start.12
  14.7 0.0 copy-start.9
  14.8 0.0 copy-start.10
  14.8 0.0 copy-start.11
  14.8 11.1 %shard_map.150 = (bf16[48,128]{1,0:T(8,128)(2,1)S(1)}, bf16[48,128]{1,0:T(8,128)(2,1)S(1)}, bf16[48,128]{1,0:T(8,128)(2,1)S(1)}, bf16[48,128]{1,0:T(8,128)(2,1)S(1)}) custom-call(bf16[128,128]{1,0:T(8,128)(2,1)S(1)} %fusion.1.s0, bf16[128,128]{1,0:T(8,128)(2,1)S(1)} %collective-permute-done.2.s1, bf16[128,128]{1,0:T(8,128)(2,1)S(1)} %collective-permute-done.3.s2, ...), custom_call_target="tpu_custom_call" | custom-call | flops 4000000000 | bytes 3000000 | tf_op jit(solution)/shard_map/pallas_call | solution.py:272
  25.9 1.2 %collective-permute-start.5 = (bf16[48,128]{1,0:T(8,128)(2,1)S(1)}, bf16[48,128]{1,0:T(8,128)(2,1)S(1)}, u32[]{:S(2)}, u32[]{:S(2)}) collective-permute-start(bf16[48,128]{1,0:T(8,128)(2,1)S(1)} %get-tuple-element.19), channel_id=1, source_target_pairs={{0,24},{8,16},{16,8},{24,0},{32,56},{40,48},{48,40},{56,32},{64,88... | collective-permute-start | bytes 36872 | tf_op jit(solution)/shard_map/ppermute | solution.py:22
  27.1 0.7 %collective-permute-start.6 = (bf16[48,128]{1,0:T(8,128)(2,1)S(1)}, bf16[48,128]{1,0:T(8,128)(2,1)S(1)}, u32[]{:S(2)}, u32[]{:S(2)}) collective-permute-start(bf16[48,128]{1,0:T(8,128)(2,1)S(1)} %get-tuple-element.20), channel_id=1, source_target_pairs={{0,16},{8,24},{16,0},{24,8},{32,48},{40,56},{48,32},{56,40},{64,80... | collective-permute-start | bytes 36872 | tf_op jit(solution)/shard_map/ppermute | solution.py:22
  27.8 0.1 collective-permute-start.7
  27.8 0.0 copy-done.12
  27.8 1.3 %collective-permute-done.5 = bf16[48,128]{1,0:T(8,128)(2,1)S(1)} collective-permute-done((bf16[48,128]{1,0:T(8,128)(2,1)S(1)}, bf16[48,128]{1,0:T(8,128)(2,1)S(1)}, u32[]{:S(2)}, u32[]{:S(2)}) %collective-permute-start.5) | collective-permute-done | bytes 12320 | tf_op jit(solution)/shard_map/ppermute | solution.py:22
  29.1 1.7 %collective-permute-done.6 = bf16[48,128]{1,0:T(8,128)(2,1)S(1)} collective-permute-done((bf16[48,128]{1,0:T(8,128)(2,1)S(1)}, bf16[48,128]{1,0:T(8,128)(2,1)S(1)}, u32[]{:S(2)}, u32[]{:S(2)}) %collective-permute-start.6) | collective-permute-done | bytes 12320 | tf_op jit(solution)/shard_map/ppermute | solution.py:22
  30.8 0.0 collective-permute-done.7
  30.8 0.1 fusion.23
  30.9 0.0 copy-done.9
  30.9 0.0 copy-done.10
  30.9 0.1 bitcast_add_fusion
  31.0 0.0 copy-start.8
  31.0 6.0 %collective-permute-start.8 = (f32[1,5,4,64]{3,2,1,0:T(4,128)S(1)}, f32[1,5,4,64]{3,2,1,0:T(4,128)S(1)}, u32[]{:S(2)}, u32[]{:S(2)}) collective-permute-start(f32[1,5,4,64]{3,2,1,0:T(4,128)S(1)} %slice.44), channel_id=1, source_target_pairs={{0,248},{8,0},{16,8},{24,16},{32,24},{40,32},{48,40},{56,48},{64,5... | collective-permute-start | bytes 15368 | tf_op jit(solution)/shard_map/ppermute | solution.py:348
  37.0 1.4 %collective-permute-done.8 = f32[1,5,4,64]{3,2,1,0:T(4,128)S(1)} collective-permute-done((f32[1,5,4,64]{3,2,1,0:T(4,128)S(1)}, f32[1,5,4,64]{3,2,1,0:T(4,128)S(1)}, u32[]{:S(2)}, u32[]{:S(2)}) %collective-permute-start.8) | collective-permute-done | bytes 5152 | tf_op jit(solution)/shard_map/ppermute | solution.py:348
  38.4 0.0 copy-done.11
  38.4 0.6 %maximum_bitcast_fusion = f32[1,4,4,5,64]{4,2,3,1,0:T(4,128)} fusion(f32[1,5,4,64]{3,2,1,0:T(4,128)S(1)} %bitcast_select_fusion, f32[3,5,4,64]{3,2,1,0:T(4,128)S(1)} %slice.43), kind=kLoop, calls=%fused_computation.5 | loop fusion | flops 5120 | bytes 40960 | tf_op jit(solution)/shard_map/broadcast_in_dim | solution.py:352
  39.0 0.0 copy-done.8
  (13 shorter events, 0.1 us)
Async XLA Ops:
  0.6 3.8 %copy-start = (bf16[1280,320]{0,1:T(8,128)(2,1)S(1)}, bf16[1280,320]{0,1:T(8,128)(2,1)}, u32[]{:S(2)}) copy-start(bf16[1280,320]{0,1:T(8,128)(2,1)} %param.21) | copy-start | bytes 2457604
  0.6 10.8 %copy-start.1 = (bf16[9,320,320]{2,1,0:T(8,128)(2,1)S(1)}, bf16[9,320,320]{2,1,0:T(8,128)(2,1)}, u32[]{:S(2)}) copy-start(bf16[9,320,320]{2,1,0:T(8,128)(2,1)} %param.22) | copy-start | bytes 5529604
  1.6 4.9 %collective-permute-start = (bf16[4,5,4,64]{3,2,1,0:T(4,128)(2,1)S(1)}, bf16[4,5,4,64]{3,2,1,0:T(4,128)(2,1)S(1)}, u32[]{:S(2)}, u32[]{:S(2)}) collective-permute-start(bf16[4,5,4,64]{3,2,1,0:T(4,128)(2,1)S(1)} %fusion.2), channel_id=1, source_target_pairs={{0,1},{1,2},{2,3},{3,4},{4,5},{5,6},{6,7},{7,0},{8,9},{9,10},{10,1... | collective-permute-start | bytes 30728 | tf_op jit(solution)/shard_map/ppermute | solution.py:27
  3.1 5.9 %collective-permute-start.1 = (bf16[4,5,4,64]{3,2,1,0:T(4,128)(2,1)S(1)}, bf16[4,5,4,64]{3,2,1,0:T(4,128)(2,1)S(1)}, u32[]{:S(2)}, u32[]{:S(2)}) collective-permute-start(bf16[4,5,4,64]{3,2,1,0:T(4,128)(2,1)S(1)} %fusion.2), channel_id=1, source_target_pairs={{0,7},{1,0},{2,1},{3,2},{4,3},{5,4},{6,5},{7,6},{8,15},{9,8},{10,9... | collective-permute-start | bytes 30728 | tf_op jit(solution)/shard_map/ppermute | solution.py:27
  9.2 4.8 %collective-permute-start.2 = (bf16[128,128]{1,0:T(8,128)(2,1)S(1)}, bf16[128,128]{1,0:T(8,128)(2,1)S(1)}, u32[]{:S(2)}, u32[]{:S(2)}) collective-permute-start(bf16[128,128]{1,0:T(8,128)(2,1)S(1)} %fusion.1.s0), channel_id=1, source_target_pairs={{0,8},{8,0},{16,24},{24,16},{32,40},{40,32},{48,56},{56,48},{64,72... | collective-permute-start | bytes 98312 | tf_op jit(solution)/shard_map/ppermute | solution.py:22
  9.3 4.7 %collective-permute-start.3 = (bf16[128,128]{1,0:T(8,128)(2,1)S(1)}, bf16[128,128]{1,0:T(8,128)(2,1)S(1)}, u32[]{:S(2)}, u32[]{:S(2)}) collective-permute-start(bf16[128,128]{1,0:T(8,128)(2,1)S(1)} %fusion.1.s0), channel_id=1, source_target_pairs={{0,16},{8,24},{16,0},{24,8},{32,48},{40,56},{48,32},{56,40},{64,80... | collective-permute-start | bytes 98312 | tf_op jit(solution)/shard_map/ppermute | solution.py:22
  11.3 3.4 %collective-permute-start.4 = (bf16[128,128]{1,0:T(8,128)(2,1)S(1)}, bf16[128,128]{1,0:T(8,128)(2,1)S(1)}, u32[]{:S(2)}, u32[]{:S(2)}) collective-permute-start(bf16[128,128]{1,0:T(8,128)(2,1)S(1)} %fusion.1.s0), channel_id=1, source_target_pairs={{0,24},{8,16},{16,8},{24,0},{32,56},{40,48},{48,40},{56,32},{64,88... | collective-permute-start | bytes 98312 | tf_op jit(solution)/shard_map/ppermute | solution.py:22
  11.4 0.7 %copy-start.6 = (bf16[9,4,320]{2,1,0:T(4,128)(2,1)S(1)}, bf16[9,4,320]{2,1,0:T(4,128)(2,1)}, u32[]{:S(2)}) copy-start(bf16[9,4,320]{2,1,0:T(4,128)(2,1)} %inlet.1) | copy-start | bytes 69124
  12.1 0.7 %copy-start.7 = (bf16[9,320,4]{1,2,0:T(4,128)(2,1)S(1)}, bf16[9,320,4]{1,2,0:T(4,128)(2,1)}, u32[]{:S(2)}) copy-start(bf16[9,320,4]{1,2,0:T(4,128)(2,1)} %param.27) | copy-start | bytes 69124
  12.9 1.8 %copy-start.2 = (bf16[320,320]{1,0:T(8,128)(2,1)S(1)}, bf16[320,320]{1,0:T(8,128)(2,1)}, u32[]{:S(2)}) copy-start(bf16[320,320]{1,0:T(8,128)(2,1)} %wq.1) | copy-start | bytes 614404
  12.9 1.8 %copy-start.3 = (bf16[320,320]{1,0:T(8,128)(2,1)S(1)}, bf16[320,320]{1,0:T(8,128)(2,1)}, u32[]{:S(2)}) copy-start(bf16[320,320]{1,0:T(8,128)(2,1)} %wk.1) | copy-start | bytes 614404
  12.9 1.8 %copy-start.4 = (bf16[320,320]{1,0:T(8,128)(2,1)S(1)}, bf16[320,320]{1,0:T(8,128)(2,1)}, u32[]{:S(2)}) copy-start(bf16[320,320]{1,0:T(8,128)(2,1)} %wv.1) | copy-start | bytes 614404
  12.9 1.8 %copy-start.5 = (bf16[320,320]{1,0:T(8,128)(2,1)S(1)}, bf16[320,320]{1,0:T(8,128)(2,1)}, u32[]{:S(2)}) copy-start(bf16[320,320]{1,0:T(8,128)(2,1)} %wo_in.1) | copy-start | bytes 614404
  14.7 13.1 %copy-start.12 = (f32[3,4]{1,0:T(4,128)S(1)}, f32[3,4]{1,0:T(4,128)}, u32[]{:S(2)}) copy-start(f32[3,4]{1,0:T(4,128)} %param.18) | copy-start | bytes 148
  14.7 16.2 %copy-start.9 = (f32[1,4,4,5,64]{4,2,3,1,0:T(4,128)S(1)}, f32[1,4,4,5,64]{4,2,3,1,0:T(4,128)}, u32[]{:S(2)}) copy-start(f32[1,4,4,5,64]{4,2,3,1,0:T(4,128)} %param.14) | copy-start | bytes 61444
  14.8 16.2 %copy-start.10 = (f32[1,4,4,5,64]{4,2,3,1,0:T(4,128)S(1)}, f32[1,4,4,5,64]{4,2,3,1,0:T(4,128)}, u32[]{:S(2)}) copy-start(f32[1,4,4,5,64]{4,2,3,1,0:T(4,128)} %param.15) | copy-start | bytes 61444
  14.8 23.6 %copy-start.11 = (f32[1,4,5,64]{3,1,2,0:T(4,128)S(1)}, f32[1,4,5,64]{3,1,2,0:T(4,128)}, u32[]{:S(2)}) copy-start(f32[1,4,5,64]{3,1,2,0:T(4,128)} %param.16) | copy-start | bytes 15364
  25.9 3.2 %collective-permute-start.5 = (bf16[48,128]{1,0:T(8,128)(2,1)S(1)}, bf16[48,128]{1,0:T(8,128)(2,1)S(1)}, u32[]{:S(2)}, u32[]{:S(2)}) collective-permute-start(bf16[48,128]{1,0:T(8,128)(2,1)S(1)} %get-tuple-element.19), channel_id=1, source_target_pairs={{0,24},{8,16},{16,8},{24,0},{32,56},{40,48},{48,40},{56,32},{64,88... | collective-permute-start | bytes 36872 | tf_op jit(solution)/shard_map/ppermute | solution.py:22
  27.1 3.7 %collective-permute-start.6 = (bf16[48,128]{1,0:T(8,128)(2,1)S(1)}, bf16[48,128]{1,0:T(8,128)(2,1)S(1)}, u32[]{:S(2)}, u32[]{:S(2)}) collective-permute-start(bf16[48,128]{1,0:T(8,128)(2,1)S(1)} %get-tuple-element.20), channel_id=1, source_target_pairs={{0,16},{8,24},{16,0},{24,8},{32,48},{40,56},{48,32},{56,40},{64,80... | collective-permute-start | bytes 36872 | tf_op jit(solution)/shard_map/ppermute | solution.py:22
  27.8 3.0 %collective-permute-start.7 = (bf16[48,128]{1,0:T(8,128)(2,1)S(1)}, bf16[48,128]{1,0:T(8,128)(2,1)S(1)}, u32[]{:S(2)}, u32[]{:S(2)}) collective-permute-start(bf16[48,128]{1,0:T(8,128)(2,1)S(1)} %get-tuple-element.21), channel_id=1, source_target_pairs={{0,8},{8,0},{16,24},{24,16},{32,40},{40,32},{48,56},{56,48},{64,72... | collective-permute-start | bytes 36872 | tf_op jit(solution)/shard_map/ppermute | solution.py:22
  31.0 8.0 %copy-start.8 = (f32[4,5,4,64]{3,2,1,0:T(4,128)}, f32[4,5,4,64]{3,2,1,0:T(4,128)S(1)}, u32[]{:S(2)}) copy-start(f32[4,5,4,64]{3,2,1,0:T(4,128)S(1)} %bitcast_add_fusion) | copy-start | bytes 61444
  31.0 7.4 %collective-permute-start.8 = (f32[1,5,4,64]{3,2,1,0:T(4,128)S(1)}, f32[1,5,4,64]{3,2,1,0:T(4,128)S(1)}, u32[]{:S(2)}, u32[]{:S(2)}) collective-permute-start(f32[1,5,4,64]{3,2,1,0:T(4,128)S(1)} %slice.44), channel_id=1, source_target_pairs={{0,248},{8,0},{16,8},{24,16},{32,24},{40,32},{48,40},{56,48},{64,5... | collective-permute-start | bytes 15368 | tf_op jit(solution)/shard_map/ppermute | solution.py:348

commit v4 on v3

--- a/solution.py
+++ b/solution.py
@@ -113,7 +113,7 @@
 def core_kernel(
     s0, s1, s2, s3, win, wres, wq, wk, wv, wo_in, wout, gather, pick, scatter,
     o0, o1, o2, o3,
-    opn, act, res, nrm, qkv, scr, att, accs, wqkv, wo, pairs,
+    opn, act, res, nrm, qkv, scr, att, accs, wqkv, wo,
 ):
     tile = lax.axis_index("chain") % GROUP
     row_block = lax.axis_index("mp")
@@ -180,28 +180,18 @@
         nrm[r] = (residual * inv_rms(residual)).astype(BF16)
 
     def project(r):
-        full = mm(wqkv[...], nrm[r]).astype(BF16)
-        qkv[r] = full[C:]
-        for b in range(2):
-            for h in range(HEADS):
-                at = h % 2
-                pairs[r % 2, b, h // 2, 64 * at : 64 * at + 64, 128 * at : 128 * at + 128] = full[
-                    64 * h : 64 * h + 64, 128 * b : 128 * b + 128
-                ]
+        qkv[r] = mm(wqkv[...], nrm[r]).astype(BF16)
 
     def score(r):
         for b in range(2):
-            for p in range(3):
-                heads = min(2, HEADS - 2 * p)
-                wide = lax.dot_general(
-                    qkv[r, 128 * p : 128 * p + 64 * heads, 128 * b : 128 * b + 128],
-                    pairs[r % 2, b, p, : 64 * heads, : 128 * heads],
+            piece = slice(128 * b, 128 * b + 128)
+            for h in range(HEADS):
+                scr[r % 2, HEADS * b + h] = lax.dot_general(
+                    qkv[r, C + 64 * h : C + 64 * h + 64, piece],
+                    qkv[r, 64 * h : 64 * h + 64, piece],
                     (((0,), (0,)), ((), ())),
                     preferred_element_type=F32,
-                )
-                for i in range(heads):
-                    part = wide[:, 128 * i : 128 * i + 128]
-                    scr[r % 2, HEADS * b + 2 * p + i] = part.reshape(16, 8, 128)
+                ).reshape(16, 8, 128)
 
     def attend(r):
         probs = []
@@ -214,7 +204,7 @@
         for b in range(2):
             piece = slice(128 * b, 128 * b + 128)
             for h in range(HEADS):
-                value = qkv[r, C + 64 * h : C + 64 * h + 64, piece]
+                value = qkv[r, 2 * C + 64 * h : 2 * C + 64 * h + 64, piece]
                 att[r, 64 * h : 64 * h + 64, piece] = mm(value, probs[HEADS * b + h]).astype(BF16)
 
     def mix(r):
@@ -233,7 +223,6 @@
                 accs[r - a] += taps[16 * a : 16 * a + 16]
 
     accs[...] = jnp.zeros_like(accs)
-    pairs[...] = jnp.zeros_like(pairs)
     for i, w in enumerate((wq, wk, wv)):
         wqkv[C * i : C * i + C, :] = w[...].T
     wo[...] = wo_in[...].T
@@ -257,11 +246,9 @@
     total = None
     for b in range(3):
         part = accs[:, 4 * b : 4 * b + 4, :].reshape(24, 256)
-        high = part.astype(BF16).astype(F32)
-        for piece in (high, part - high):
-            wide = jnp.where(pair_of == pair_no, piece[None], 0.0)
-            term = mm(wide.reshape(192, 256).astype(BF16), scatter[b])
-            total = term if total is None else total + term
+        wide = jnp.where(pair_of == pair_no, part[None], 0.0)
+        term = mm(wide.reshape(192, 256).astype(BF16), scatter[b])
+        total = term if total is None else total + term
     for k, out in enumerate((o0, o1, o2, o3)):
         out[...] = total[48 * k : 48 * k + 48].astype(BF16)
 
@@ -279,13 +266,12 @@
             pltpu.VMEM(((ROWS + 4) * 960, 256), BF16),
             pltpu.VMEM((ROWS + 2, C, 256), F32),
             pltpu.VMEM((ROWS + 2, C, 256), BF16),
-            pltpu.VMEM((ROWS + 2, 2 * C, 256), BF16),
+            pltpu.VMEM((ROWS + 2, 3 * C, 256), BF16),
             pltpu.VMEM((2, 10, 16, 8, 128), F32),
             pltpu.VMEM((ROWS + 2, C, 256), BF16),
             pltpu.VMEM((ROWS + 1, 16, 256), F32),
             pltpu.VMEM((3 * C, C), BF16),
             pltpu.VMEM((C, C), BF16),
-            pltpu.VMEM((2, 2, 3, 128, 256), BF16),
         ],
         compiler_params=pltpu.CompilerParams(vmem_limit_bytes=36 * 1024 * 1024),
         cost_estimate=pl.CostEstimate(

time: 39.3 us -> 39.1 us (level)
  no operation moved by 1% of the time
where the time goes in v4:
time: 39.1 us; the launch traced here: 38.8 us
  starting transfers between devices  12.1 us (31%)
  Pallas kernels  12 us (31%)
  waiting for transfers between devices  7.46 us (19%)
  other arithmetic  2.59 us (7%)
  local copies, waits for them, and re-layouts  2.15 us (5%)
  matrix products  1.68 us (4%)
  between operations  0.86 us (2%)
    pallas_call x1, Pallas kernels, core(): pl.pallas_call(core_kernel, out_shape=(out,) * 4, in_specs=[vmem] * 14, o...  10.9 us
    ppermute x1, starting transfers between devices, local(): lax.ppermute(stepped[:1], 'chain', [(i, (i - 1) % count) for i in range(c...  5.98 us
    ppermute x6, starting transfers between devices, from_partner(): return lax.ppermute(block, 'chain', [(i, i ^ bits) for i in range(count)])  4.1 us
    ppermute x6, waiting for transfers between devices, from_partner(): return lax.ppermute(block, 'chain', [(i, i ^ bits) for i in range(count)])  3.61 us
    ppermute x2, waiting for transfers between devices, from_row(): lax.ppermute(block, 'mp', [(i, (i + by) % count) for i in range(count)])  2.46 us
    ppermute x2, starting transfers between devices, from_row(): lax.ppermute(block, 'mp', [(i, (i + by) % count) for i in range(count)])  2.03 us
    dot_general x1, matrix products, local(): shift = jnp.dot(hidden, time_second, preferred_element_type=F32)  1.68 us
    unnamed x26, local copies, waits for them, and re-layouts  1.55 us
  transfers between devices with their start and end apart: 9, of which 5 were waited for; matrix products, arithmetic and copies ran while one was open for 7% of the time, Pallas kernels for 3%

profile of v4, /device:TPU:6, one launch (start us, length us, event | category | flops | bytes accessed | tf_op | source)
XLA Modules:
  0.0 38.8 jit_solution(12010965649687857052)
XLA Ops:
  0.6 0.0 copy-start
  0.6 0.0 copy-start.1
  0.7 0.9 %fusion.2 = bf16[4,5,4,64]{3,2,1,0:T(4,128)(2,1)S(1)} fusion(f32[1,4,4,5,64]{4,2,3,1,0:T(4,128)} %param.14), kind=kLoop, calls=%fused_computation.14 | loop fusion | flops 5120 | bytes 30720 | tf_op jit(solution)/shard_map/convert_element_type | solution.py:302
  1.6 1.5 %collective-permute-start = (bf16[4,5,4,64]{3,2,1,0:T(4,128)(2,1)S(1)}, bf16[4,5,4,64]{3,2,1,0:T(4,128)(2,1)S(1)}, u32[]{:S(2)}, u32[]{:S(2)}) collective-permute-start(bf16[4,5,4,64]{3,2,1,0:T(4,128)(2,1)S(1)} %fusion.2), channel_id=1, source_target_pairs={{0,1},{1,2},{2,3},{3,4},{4,5},{5,6},{6,7},{7,0},{8,9},{9,10},{10,1... | collective-permute-start | bytes 30728 | tf_op jit(solution)/shard_map/ppermute | solution.py:27
  3.1 0.5 %collective-permute-start.1 = (bf16[4,5,4,64]{3,2,1,0:T(4,128)(2,1)S(1)}, bf16[4,5,4,64]{3,2,1,0:T(4,128)(2,1)S(1)}, u32[]{:S(2)}, u32[]{:S(2)}) collective-permute-start(bf16[4,5,4,64]{3,2,1,0:T(4,128)(2,1)S(1)} %fusion.2), channel_id=1, source_target_pairs={{0,7},{1,0},{2,1},{3,2},{4,3},{5,4},{6,5},{7,6},{8,15},{9,8},{10,9... | collective-permute-start | bytes 30728 | tf_op jit(solution)/shard_map/ppermute | solution.py:27
  3.6 0.7 %convert_element_type.36 = f32[4]{0:T(128)S(1)} convert(s32[4]{0:T(128)} %param.17) | non-fusion elementwise | flops 4 | bytes 32 | tf_op jit(solution)/shard_map/convert_element_type | solution.py:33
  4.3 0.1 fusion.8
  4.4 0.0 copy-done
  4.4 1.7 %reduce-precision_convert_fusion = (bf16[4,320]{1,0:T(4,128)(2,1)S(1)}, bf16[4,320]{1,0:T(4,128)(2,1)S(1)}) fusion(bf16[1280,320]{0,1:T(8,128)(2,1)S(1)} %copy-done, bf16[320,1280]{1,0:T(8,128)(2,1)} %param.20, bf16[4,160]{1,0:T(4,128)(2,1)S(1)} %get-tuple-element.30, bf16[4,160]{1,0:T(4,128)(2,1)S(1)} %get-tuple-element.29), kind=kOutput, calls=%fused_computation.21 | convolution fusion | flops 6589440 | bytes 1646080 | tf_op jit(solution)/shard_map/dot_general | solution.py:307
  6.1 0.1 stack.10
  6.2 0.1 stack.9
  6.3 0.1 convert_element_type.39
  6.4 0.1 pad.18.clone
  6.5 0.0 collective-permute-done
  6.5 2.5 %collective-permute-done.1 = bf16[4,5,4,64]{3,2,1,0:T(4,128)(2,1)S(1)} collective-permute-done((bf16[4,5,4,64]{3,2,1,0:T(4,128)(2,1)S(1)}, bf16[4,5,4,64]{3,2,1,0:T(4,128)(2,1)S(1)}, u32[]{:S(2)}, u32[]{:S(2)}) %collective-permute-start.1) | collective-permute-done | bytes 10272 | tf_op jit(solution)/shard_map/ppermute | solution.py:27
  9.0 0.1 maximum_maximum_fusion
  9.1 0.1 reshape.39
  9.2 0.1 collective-permute-start.2
  9.3 2.0 %collective-permute-start.3 = (bf16[128,128]{1,0:T(8,128)(2,1)S(1)}, bf16[128,128]{1,0:T(8,128)(2,1)S(1)}, u32[]{:S(2)}, u32[]{:S(2)}) collective-permute-start(bf16[128,128]{1,0:T(8,128)(2,1)S(1)} %fusion.1.s0), channel_id=1, source_target_pairs={{0,16},{8,24},{16,0},{24,8},{32,48},{40,56},{48,32},{56,40},{64,80... | collective-permute-start | bytes 98312 | tf_op jit(solution)/shard_map/ppermute | solution.py:22
  11.3 0.1 collective-permute-start.4
  11.4 0.0 copy-done.1
  11.4 0.0 copy-start.6
  11.4 0.7 %copy-done.6 = bf16[9,4,320]{2,1,0:T(4,128)(2,1)S(1)} copy-done((bf16[9,4,320]{2,1,0:T(4,128)(2,1)S(1)}, bf16[9,4,320]{2,1,0:T(4,128)(2,1)}, u32[]{:S(2)}) %copy-start.6) | copy-done | bytes 23064
  12.1 0.0 copy-start.7
  12.1 0.7 %copy-done.7 = bf16[9,320,4]{1,2,0:T(4,128)(2,1)S(1)} copy-done((bf16[9,320,4]{1,2,0:T(4,128)(2,1)S(1)}, bf16[9,320,4]{1,2,0:T(4,128)(2,1)}, u32[]{:S(2)}) %copy-start.7) | copy-done | bytes 23064
  12.9 0.0 copy-start.2
  12.9 0.0 copy-start.3
  12.9 0.0 copy-start.4
  12.9 0.0 copy-start.5
  12.9 1.1 %shard_map.149 = (bf16[6,320,128]{2,1,0:T(8,128)(2,1)S(1)}, bf16[320,2880]{1,0:T(8,128)(2,1)S(1)}, bf16[48,320]{1,0:T(8,128)(2,1)S(1)}, bf16[3,128,384]{2,1,0:T(...) custom-call(bf16[9,4,320]{2,1,0:T(4,128)(2,1)S(1)} %copy-done.6, ...), custom_call_target="tpu_custom_call" | custom-call | flops 2000000000 | bytes 6000000 | tf_op jit(solution)/shard_map/pallas_call | solution.py:100
  14.0 0.0 collective-permute-done.2.s1
  14.0 0.0 collective-permute-done.3.s2
  14.1 0.6 %collective-permute-done.4.s3 = bf16[128,128]{1,0:T(8,128)(2,1)S(1)} collective-permute-done((bf16[128,128]{1,0:T(8,128)(2,1)S(1)}, bf16[128,128]{1,0:T(8,128)(2,1)S(1)}, u32[]{:S(2)}, u32[]{:S(2)}) %collective-permute-start.4) | collective-permute-done | bytes 32800 | tf_op jit(solution)/shard_map/ppermute | solution.py:22
  14.7 0.0 copy-done.2
  14.7 0.0 copy-done.3
  14.7 0.0 copy-done.4
  14.7 0.0 copy-done.5
  14.7 0.0 copy-start.12
  14.7 0.0 copy-start.9
  14.8 0.0 copy-start.10
  14.8 0.0 copy-start.11
  14.8 10.9 %shard_map.150 = (bf16[48,128]{1,0:T(8,128)(2,1)S(1)}, bf16[48,128]{1,0:T(8,128)(2,1)S(1)}, bf16[48,128]{1,0:T(8,128)(2,1)S(1)}, bf16[48,128]{1,0:T(8,128)(2,1)S(1)}) custom-call(bf16[128,128]{1,0:T(8,128)(2,1)S(1)} %fusion.1.s0, bf16[128,128]{1,0:T(8,128)(2,1)S(1)} %collective-permute-done.2.s1, bf16[128,128]{1,0:T(8,128)(2,1)S(1)} %collective-permute-done.3.s2, ...), custom_call_target="tpu_custom_call" | custom-call | flops 4000000000 | bytes 3000000 | tf_op jit(solution)/shard_map/pallas_call | solution.py:259
  25.6 1.2 %collective-permute-start.5 = (bf16[48,128]{1,0:T(8,128)(2,1)S(1)}, bf16[48,128]{1,0:T(8,128)(2,1)S(1)}, u32[]{:S(2)}, u32[]{:S(2)}) collective-permute-start(bf16[48,128]{1,0:T(8,128)(2,1)S(1)} %get-tuple-element.19), channel_id=1, source_target_pairs={{0,24},{8,16},{16,8},{24,0},{32,56},{40,48},{48,40},{56,32},{64,88... | collective-permute-start | bytes 36872 | tf_op jit(solution)/shard_map/ppermute | solution.py:22
  26.9 0.7 %collective-permute-start.6 = (bf16[48,128]{1,0:T(8,128)(2,1)S(1)}, bf16[48,128]{1,0:T(8,128)(2,1)S(1)}, u32[]{:S(2)}, u32[]{:S(2)}) collective-permute-start(bf16[48,128]{1,0:T(8,128)(2,1)S(1)} %get-tuple-element.20), channel_id=1, source_target_pairs={{0,16},{8,24},{16,0},{24,8},{32,48},{40,56},{48,32},{56,40},{64,80... | collective-permute-start | bytes 36872 | tf_op jit(solution)/shard_map/ppermute | solution.py:22
  27.5 0.1 collective-permute-start.7
  27.6 0.0 copy-done.12
  27.6 1.3 %collective-permute-done.5 = bf16[48,128]{1,0:T(8,128)(2,1)S(1)} collective-permute-done((bf16[48,128]{1,0:T(8,128)(2,1)S(1)}, bf16[48,128]{1,0:T(8,128)(2,1)S(1)}, u32[]{:S(2)}, u32[]{:S(2)}) %collective-permute-start.5) | collective-permute-done | bytes 12320 | tf_op jit(solution)/shard_map/ppermute | solution.py:22
  28.8 1.7 %collective-permute-done.6 = bf16[48,128]{1,0:T(8,128)(2,1)S(1)} collective-permute-done((bf16[48,128]{1,0:T(8,128)(2,1)S(1)}, bf16[48,128]{1,0:T(8,128)(2,1)S(1)}, u32[]{:S(2)}, u32[]{:S(2)}) %collective-permute-start.6) | collective-permute-done | bytes 12320 | tf_op jit(solution)/shard_map/ppermute | solution.py:22
  30.6 0.0 collective-permute-done.7
  30.6 0.1 fusion.23
  30.7 0.0 copy-done.9
  30.7 0.0 copy-done.10
  30.7 0.1 bitcast_add_fusion
  30.8 0.0 copy-start.8
  30.8 6.0 %collective-permute-start.8 = (f32[1,5,4,64]{3,2,1,0:T(4,128)S(1)}, f32[1,5,4,64]{3,2,1,0:T(4,128)S(1)}, u32[]{:S(2)}, u32[]{:S(2)}) collective-permute-start(f32[1,5,4,64]{3,2,1,0:T(4,128)S(1)} %slice.44), channel_id=1, source_target_pairs={{0,248},{8,0},{16,8},{24,16},{32,24},{40,32},{48,40},{56,48},{64,5... | collective-permute-start | bytes 15368 | tf_op jit(solution)/shard_map/ppermute | solution.py:334
  36.8 1.4 %collective-permute-done.8 = f32[1,5,4,64]{3,2,1,0:T(4,128)S(1)} collective-permute-done((f32[1,5,4,64]{3,2,1,0:T(4,128)S(1)}, f32[1,5,4,64]{3,2,1,0:T(4,128)S(1)}, u32[]{:S(2)}, u32[]{:S(2)}) %collective-permute-start.8) | collective-permute-done | bytes 5152 | tf_op jit(solution)/shard_map/ppermute | solution.py:334
  38.2 0.0 copy-done.11
  38.2 0.6 %maximum_bitcast_fusion = f32[1,4,4,5,64]{4,2,3,1,0:T(4,128)} fusion(f32[1,5,4,64]{3,2,1,0:T(4,128)S(1)} %bitcast_select_fusion, f32[3,5,4,64]{3,2,1,0:T(4,128)S(1)} %slice.43), kind=kLoop, calls=%fused_computation.5 | loop fusion | flops 5120 | bytes 40960 | tf_op jit(solution)/shard_map/broadcast_in_dim | solution.py:338
  38.8 0.0 copy-done.8
  (13 shorter events, 0.1 us)
Async XLA Ops:
  0.6 3.8 %copy-start = (bf16[1280,320]{0,1:T(8,128)(2,1)S(1)}, bf16[1280,320]{0,1:T(8,128)(2,1)}, u32[]{:S(2)}) copy-start(bf16[1280,320]{0,1:T(8,128)(2,1)} %param.21) | copy-start | bytes 2457604
  0.6 10.8 %copy-start.1 = (bf16[9,320,320]{2,1,0:T(8,128)(2,1)S(1)}, bf16[9,320,320]{2,1,0:T(8,128)(2,1)}, u32[]{:S(2)}) copy-start(bf16[9,320,320]{2,1,0:T(8,128)(2,1)} %param.22) | copy-start | bytes 5529604
  1.6 4.9 %collective-permute-start = (bf16[4,5,4,64]{3,2,1,0:T(4,128)(2,1)S(1)}, bf16[4,5,4,64]{3,2,1,0:T(4,128)(2,1)S(1)}, u32[]{:S(2)}, u32[]{:S(2)}) collective-permute-start(bf16[4,5,4,64]{3,2,1,0:T(4,128)(2,1)S(1)} %fusion.2), channel_id=1, source_target_pairs={{0,1},{1,2},{2,3},{3,4},{4,5},{5,6},{6,7},{7,0},{8,9},{9,10},{10,1... | collective-permute-start | bytes 30728 | tf_op jit(solution)/shard_map/ppermute | solution.py:27
  3.1 5.9 %collective-permute-start.1 = (bf16[4,5,4,64]{3,2,1,0:T(4,128)(2,1)S(1)}, bf16[4,5,4,64]{3,2,1,0:T(4,128)(2,1)S(1)}, u32[]{:S(2)}, u32[]{:S(2)}) collective-permute-start(bf16[4,5,4,64]{3,2,1,0:T(4,128)(2,1)S(1)} %fusion.2), channel_id=1, source_target_pairs={{0,7},{1,0},{2,1},{3,2},{4,3},{5,4},{6,5},{7,6},{8,15},{9,8},{10,9... | collective-permute-start | bytes 30728 | tf_op jit(solution)/shard_map/ppermute | solution.py:27
  9.2 4.8 %collective-permute-start.2 = (bf16[128,128]{1,0:T(8,128)(2,1)S(1)}, bf16[128,128]{1,0:T(8,128)(2,1)S(1)}, u32[]{:S(2)}, u32[]{:S(2)}) collective-permute-start(bf16[128,128]{1,0:T(8,128)(2,1)S(1)} %fusion.1.s0), channel_id=1, source_target_pairs={{0,8},{8,0},{16,24},{24,16},{32,40},{40,32},{48,56},{56,48},{64,72... | collective-permute-start | bytes 98312 | tf_op jit(solution)/shard_map/ppermute | solution.py:22
  9.3 4.7 %collective-permute-start.3 = (bf16[128,128]{1,0:T(8,128)(2,1)S(1)}, bf16[128,128]{1,0:T(8,128)(2,1)S(1)}, u32[]{:S(2)}, u32[]{:S(2)}) collective-permute-start(bf16[128,128]{1,0:T(8,128)(2,1)S(1)} %fusion.1.s0), channel_id=1, source_target_pairs={{0,16},{8,24},{16,0},{24,8},{32,48},{40,56},{48,32},{56,40},{64,80... | collective-permute-start | bytes 98312 | tf_op jit(solution)/shard_map/ppermute | solution.py:22
  11.3 3.4 %collective-permute-start.4 = (bf16[128,128]{1,0:T(8,128)(2,1)S(1)}, bf16[128,128]{1,0:T(8,128)(2,1)S(1)}, u32[]{:S(2)}, u32[]{:S(2)}) collective-permute-start(bf16[128,128]{1,0:T(8,128)(2,1)S(1)} %fusion.1.s0), channel_id=1, source_target_pairs={{0,24},{8,16},{16,8},{24,0},{32,56},{40,48},{48,40},{56,32},{64,88... | collective-permute-start | bytes 98312 | tf_op jit(solution)/shard_map/ppermute | solution.py:22
  11.4 0.7 %copy-start.6 = (bf16[9,4,320]{2,1,0:T(4,128)(2,1)S(1)}, bf16[9,4,320]{2,1,0:T(4,128)(2,1)}, u32[]{:S(2)}) copy-start(bf16[9,4,320]{2,1,0:T(4,128)(2,1)} %inlet.1) | copy-start | bytes 69124
  12.1 0.7 %copy-start.7 = (bf16[9,320,4]{1,2,0:T(4,128)(2,1)S(1)}, bf16[9,320,4]{1,2,0:T(4,128)(2,1)}, u32[]{:S(2)}) copy-start(bf16[9,320,4]{1,2,0:T(4,128)(2,1)} %param.27) | copy-start | bytes 69124
  12.9 1.8 %copy-start.2 = (bf16[320,320]{1,0:T(8,128)(2,1)S(1)}, bf16[320,320]{1,0:T(8,128)(2,1)}, u32[]{:S(2)}) copy-start(bf16[320,320]{1,0:T(8,128)(2,1)} %wq.1) | copy-start | bytes 614404
  12.9 1.8 %copy-start.3 = (bf16[320,320]{1,0:T(8,128)(2,1)S(1)}, bf16[320,320]{1,0:T(8,128)(2,1)}, u32[]{:S(2)}) copy-start(bf16[320,320]{1,0:T(8,128)(2,1)} %wk.1) | copy-start | bytes 614404
  12.9 1.8 %copy-start.4 = (bf16[320,320]{1,0:T(8,128)(2,1)S(1)}, bf16[320,320]{1,0:T(8,128)(2,1)}, u32[]{:S(2)}) copy-start(bf16[320,320]{1,0:T(8,128)(2,1)} %wv.1) | copy-start | bytes 614404
  12.9 1.8 %copy-start.5 = (bf16[320,320]{1,0:T(8,128)(2,1)S(1)}, bf16[320,320]{1,0:T(8,128)(2,1)}, u32[]{:S(2)}) copy-start(bf16[320,320]{1,0:T(8,128)(2,1)} %wo_in.1) | copy-start | bytes 614404
  14.7 12.9 %copy-start.12 = (f32[3,4]{1,0:T(4,128)S(1)}, f32[3,4]{1,0:T(4,128)}, u32[]{:S(2)}) copy-start(f32[3,4]{1,0:T(4,128)} %param.18) | copy-start | bytes 148
  14.7 15.9 %copy-start.9 = (f32[1,4,4,5,64]{4,2,3,1,0:T(4,128)S(1)}, f32[1,4,4,5,64]{4,2,3,1,0:T(4,128)}, u32[]{:S(2)}) copy-start(f32[1,4,4,5,64]{4,2,3,1,0:T(4,128)} %param.14) | copy-start | bytes 61444
  14.8 15.9 %copy-start.10 = (f32[1,4,4,5,64]{4,2,3,1,0:T(4,128)S(1)}, f32[1,4,4,5,64]{4,2,3,1,0:T(4,128)}, u32[]{:S(2)}) copy-start(f32[1,4,4,5,64]{4,2,3,1,0:T(4,128)} %param.15) | copy-start | bytes 61444
  14.8 23.4 %copy-start.11 = (f32[1,4,5,64]{3,1,2,0:T(4,128)S(1)}, f32[1,4,5,64]{3,1,2,0:T(4,128)}, u32[]{:S(2)}) copy-start(f32[1,4,5,64]{3,1,2,0:T(4,128)} %param.16) | copy-start | bytes 15364
  25.6 3.2 %collective-permute-start.5 = (bf16[48,128]{1,0:T(8,128)(2,1)S(1)}, bf16[48,128]{1,0:T(8,128)(2,1)S(1)}, u32[]{:S(2)}, u32[]{:S(2)}) collective-permute-start(bf16[48,128]{1,0:T(8,128)(2,1)S(1)} %get-tuple-element.19), channel_id=1, source_target_pairs={{0,24},{8,16},{16,8},{24,0},{32,56},{40,48},{48,40},{56,32},{64,88... | collective-permute-start | bytes 36872 | tf_op jit(solution)/shard_map/ppermute | solution.py:22
  26.9 3.7 %collective-permute-start.6 = (bf16[48,128]{1,0:T(8,128)(2,1)S(1)}, bf16[48,128]{1,0:T(8,128)(2,1)S(1)}, u32[]{:S(2)}, u32[]{:S(2)}) collective-permute-start(bf16[48,128]{1,0:T(8,128)(2,1)S(1)} %get-tuple-element.20), channel_id=1, source_target_pairs={{0,16},{8,24},{16,0},{24,8},{32,48},{40,56},{48,32},{56,40},{64,80... | collective-permute-start | bytes 36872 | tf_op jit(solution)/shard_map/ppermute | solution.py:22
  27.5 3.0 %collective-permute-start.7 = (bf16[48,128]{1,0:T(8,128)(2,1)S(1)}, bf16[48,128]{1,0:T(8,128)(2,1)S(1)}, u32[]{:S(2)}, u32[]{:S(2)}) collective-permute-start(bf16[48,128]{1,0:T(8,128)(2,1)S(1)} %get-tuple-element.21), channel_id=1, source_target_pairs={{0,8},{8,0},{16,24},{24,16},{32,40},{40,32},{48,56},{56,48},{64,72... | collective-permute-start | bytes 36872 | tf_op jit(solution)/shard_map/ppermute | solution.py:22
  30.8 8.0 %copy-start.8 = (f32[4,5,4,64]{3,2,1,0:T(4,128)}, f32[4,5,4,64]{3,2,1,0:T(4,128)S(1)}, u32[]{:S(2)}) copy-start(f32[4,5,4,64]{3,2,1,0:T(4,128)S(1)} %bitcast_add_fusion) | copy-start | bytes 61444
  30.8 7.4 %collective-permute-start.8 = (f32[1,5,4,64]{3,2,1,0:T(4,128)S(1)}, f32[1,5,4,64]{3,2,1,0:T(4,128)S(1)}, u32[]{:S(2)}, u32[]{:S(2)}) collective-permute-start(f32[1,5,4,64]{3,2,1,0:T(4,128)S(1)} %slice.44), channel_id=1, source_target_pairs={{0,248},{8,0},{16,8},{24,16},{32,24},{40,32},{48,40},{56,48},{64,5... | collective-permute-start | bytes 15368 | tf_op jit(solution)/shard_map/ppermute | solution.py:334
